TPU v7x, 256 devices: a whole 4x4x8 slice. The times are simulated.
256 devices in a mesh: tm: 16 (over y, x_hi, core), space: 16 (over x_lo, z).
Axes of the slice: x: 4 (x_hi: 2, x_lo: 2; x = x_hi * 2 + x_lo), y: 4, z: 8, core: 2. Of those that a mesh axis runs over, the one named last changes fastest.
Arguments:
- adjoint_iterate: float32 [128, 16, 128, 128], P('tm', None, 'space'), may hold values from -6 to 6
- innovations: float32 [128, 16, 2048], P('tm', None, 'space'), may hold values from -6 to 6
- station_cells: int32 [128, 2048], P('tm', 'space'), may hold values from 0 to 1023
- diffusivity: float32 [16, 128, 128], P(None, 'space'), may hold values from 0.01 to 0.08
- wind_x: float32 [16, 128, 128], P(None, 'space'), may hold values from -0.2 to 0.2
- wind_y: float32 [16, 128, 128], P(None, 'space'), may hold values from -0.2 to 0.2
- vertical_mixing: float32 [16, 128, 128], P(None, 'space'), may hold values from 0.01 to 0.1
Outputs:
- updated_iterate: float32 [128, 16, 128, 128], P('tm', None, 'space')
Inputs may be any that keep to these rules, and one draw needn't show every extreme that they name: `station_cells`: A station's column within its tile of 8 x 128 columns is numbered x * 128 + y; several stations may share a column.
All inputs are finite; a program needn't handle non-finite values.
Results may differ from a plain program's by a relative error of at most 0.0003.
Values sent between devices are 32-bit elements; how exact they have to be, the bound alone decides.
A program may use at most 64 MiB of HBM per device.

v0:
```python
import math

import jax
import jax.numpy as jnp
from jax import lax
from jax.sharding import PartitionSpec as P

LEV = 16
TX = 8
NY = 128
STEPS_DEV = 8
INNER = 4


circ_alpha = 0.1


def from_behind(value, axis, steps):
    count = lax.axis_size(axis)
    leading, last = (max(0, -steps), min(count, count - steps))
    return lax.ppermute(value, axis, [(source, source + steps) for source in range(leading, last)])


def with_halo(cells, sides, width):
    for axis, dim in sides:
        count = lax.axis_size(axis)
        ends = count - 1
        head = lax.slice_in_dim(cells, 0, width, axis=dim)
        tail = lax.slice_in_dim(cells, cells.shape[dim] - width, cells.shape[dim], axis=dim)
        cells = jnp.concatenate(
            [
                lax.ppermute(tail, axis, [(i, (i + 1) % count) for i in range(ends)]),
                cells,
                lax.ppermute(head, axis, [((i + 1) % count, i) for i in range(ends)]),
            ],
            axis=dim,
        )
    return cells


def transfer_rates(diffusivity, wind_x, wind_y, vertical_mixing):
    east_rate = diffusivity + jnp.maximum(-wind_x, 0.0)
    west_rate = diffusivity + jnp.maximum(wind_x, 0.0)
    north_rate = diffusivity + jnp.maximum(-wind_y, 0.0)
    south_rate = diffusivity + jnp.maximum(wind_y, 0.0)
    return jnp.stack(
        [east_rate, west_rate, north_rate, south_rate, vertical_mixing, vertical_mixing]
    )


def apply_transpose(padded, rates_pad, retained):
    center = padded[..., 1:-1, 1:-1, 1:-1]
    summed = retained * center
    summed = summed + rates_pad[0, 1:-1, :-2, 1:-1] * padded[..., 1:-1, :-2, 1:-1]
    summed = summed + rates_pad[1, 1:-1, 2:, 1:-1] * padded[..., 1:-1, 2:, 1:-1]
    summed = summed + rates_pad[2, 1:-1, 1:-1, :-2] * padded[..., 1:-1, 1:-1, :-2]
    summed = summed + rates_pad[3, 1:-1, 1:-1, 2:] * padded[..., 1:-1, 1:-1, 2:]
    summed = summed + rates_pad[4, :-2, 1:-1, 1:-1] * padded[..., :-2, 1:-1, 1:-1]
    summed = summed + rates_pad[5, 2:, 1:-1, 1:-1] * padded[..., 2:, 1:-1, 1:-1]
    return summed


def fourier_tables(horizon):
    freq_rows = jnp.arange(horizon, dtype=jnp.int32)
    phase_int = freq_rows[:, None] * freq_rows[None, :] % horizon
    angles = phase_int.astype(jnp.float32) * (2.0 * math.pi / horizon)
    return (jnp.cos(angles), jnp.sin(angles))


def rotation(horizon, freq_count):
    freq_rows = jnp.arange(freq_count, dtype=jnp.int32)
    angles = freq_rows.astype(jnp.float32) * (2.0 * math.pi / horizon)
    return (jnp.cos(angles)[:, None, None, None], jnp.sin(angles)[:, None, None, None])


def rotate_step(source, applied, cos_freq, sin_freq, beta_step):
    real_part = source[0] + beta_step * (cos_freq * applied[0] - sin_freq * applied[1])
    imag_part = source[1] + beta_step * (sin_freq * applied[0] + cos_freq * applied[1])
    return jnp.stack([real_part, imag_part])


def matmul_exact(table, rows):
    return jnp.dot(table, rows, precision=lax.Precision.HIGHEST)


def body(adjoint_iterate, innovations, station_cells, diffusivity, wind_x, wind_y, vertical_mixing):
    time_parts = lax.axis_size("tm")
    horizon = STEPS_DEV * time_parts
    levels_local = LEV // time_parts
    time_rank = lax.axis_index("tm")
    rate_fields = transfer_rates(diffusivity, wind_x, wind_y, vertical_mixing)
    retained = 1.0 - jnp.sum(rate_fields, axis=0)

    def scatter_step(cell_ids, values):
        return jnp.zeros((LEV, TX * NY), jnp.float32).at[:, cell_ids].add(values)

    forcing = jax.vmap(scatter_step)(station_cells, innovations).reshape(STEPS_DEV, LEV, TX, NY)
    leading = from_behind(adjoint_iterate[:1], "tm", -1)
    following = jnp.concatenate([adjoint_iterate[1:], leading], axis=0)
    extended = with_halo(jnp.concatenate([rate_fields, following], axis=0), (("space", 2),), 1)
    extended = jnp.pad(extended, ((0, 0), (1, 1), (0, 0), (1, 1)))
    rates_pad = extended[:6]
    residual = forcing - adjoint_iterate + apply_transpose(extended[6:], rates_pad, retained)
    log_beta = math.log(circ_alpha) / horizon
    beta_step = math.exp(log_beta)
    step_global = (time_rank * STEPS_DEV + jnp.arange(STEPS_DEV, dtype=jnp.int32)).astype(
        jnp.float32
    )
    scaled = residual * jnp.exp(-step_global * log_beta)[:, None, None, None]
    gathered = lax.all_to_all(scaled, "tm", split_axis=1, concat_axis=0, tiled=True)
    flat_rows = gathered.reshape(horizon, -1)
    cos_table, sin_table = fourier_tables(horizon)
    real_src = matmul_exact(cos_table, flat_rows)
    imag_src = -matmul_exact(sin_table, flat_rows)
    source = jnp.stack([real_src, imag_src]).reshape(2, horizon, levels_local, TX, NY)
    cos_freq, sin_freq = rotation(horizon, horizon)
    level_start = time_rank * levels_local
    local_rates = lax.dynamic_slice_in_dim(rates_pad, level_start, levels_local + 2, 1)
    local_retained = lax.dynamic_slice_in_dim(retained, level_start, levels_local, 0)
    iterate = source
    for sweep_index in range(INNER):
        padded = with_halo(iterate, (("tm", 2), ("space", 3)), 1)
        padded = jnp.pad(padded, ((0, 0), (0, 0), (0, 0), (0, 0), (1, 1)))
        applied = apply_transpose(padded, local_rates, local_retained)
        iterate = rotate_step(source, applied, cos_freq, sin_freq, beta_step)
    real_rows = iterate[0].reshape(horizon, -1)
    imag_rows = iterate[1].reshape(horizon, -1)
    restored = (matmul_exact(cos_table, real_rows) - matmul_exact(sin_table, imag_rows)) / horizon
    restored = restored.reshape(horizon, levels_local, TX, NY)
    returned = lax.all_to_all(restored, "tm", split_axis=0, concat_axis=1, tiled=True)
    correction = returned * jnp.exp(step_global * log_beta)[:, None, None, None]
    return adjoint_iterate + correction


def solution(mesh):
    in_specs = (
        P("tm", None, "space", None),
        P("tm", None, "space"),
        P("tm", "space"),
        P(None, "space", None),
        P(None, "space", None),
        P(None, "space", None),
        P(None, "space", None),
    )
    out_specs = P("tm", None, "space", None)
    return jax.shard_map(body, mesh=mesh, in_specs=in_specs, out_specs=out_specs, check_vma=False)
```

profile of v0, /device:TPU:3, one launch (start us, length us, event | category | flops | bytes accessed | tf_op | source)
XLA Modules:
  0.0 312.1 jit_solution(3323740578238665612)
XLA Ops:
  1.2 2.6 collective-permute-start
  6.2 1.6 fusion.77
  14.8 3.5 %collective-permute-start.1 = (f32[14,16,1,128]{3,1,2,0:T(8,128)S(1)}, f32[14,16,1,128]{3,1,2,0:T(8,128)S(1)}, u32[]{:S(2)}, u32[]{:S(2)}) collective-permute-start(f32[14,16,1,128]{3,1,2,0:T(8,128)S(1)} %get-tuple-element.33), channel_id=1, source_target_pairs={{0,1},{1,2},{2,3},{3,4},{4,5},{5,6},{6,7},{7,8},{8,9},{9,10},{10,1... | collective-permute-start | bytes 344072 | tf_op jit(solution)/shard_map/ppermute | solution.py:32
  18.3 5.8 %collective-permute-start.2 = (f32[14,16,1,128]{3,1,2,0:T(8,128)S(1)}, f32[14,16,1,128]{3,1,2,0:T(8,128)}, u32[]{:S(2)}, u32[]{:S(2)}) collective-permute-start(f32[14,16,1,128]{3,1,2,0:T(8,128)S(1)} %get-tuple-element.34), channel_id=1, source_target_pairs={{1,0},{2,1},{3,2},{4,3},{5,4},{6,5},{7,6},{8,7},{9,8},{10,9},{11,1... | collective-permute-start | bytes 344072 | tf_op jit(solution)/shard_map/ppermute | solution.py:34
  25.2 8.2 %scatter_custom_fusion = f32[8192,16]{1,0:T(8,128)} fusion(s32[1024]{0:T(1024)S(1)} %select_bitcast_fusion, f32[1024,16]{1,0:T(8,128)S(1)} %bitcast.122, f32[]{:T(128)} %constant.19.clone.1), kind=kCustom, calls=%fused_computation.32 | custom fusion | flops 16384 | bytes 524292
  33.4 3.5 %copy.43 = f32[8,1024,16]{1,0,2:T(8,128)} copy(f32[8,1024,16]{2,1,0:T(8,128)} %bitcast.103) | data formatting | bytes 1048576
  37.0 2.6 select_maximum_fusion.19
  40.6 2.4 fusion.54
  43.2 18.3 %all_to_all.33 = f32[8,16,8,128]{3,2,0,1:T(8,128)S(1)} all-to-all(f32[8,16,8,128]{3,2,0,1:T(8,128)S(1)} %copy.38), channel_id=1, replica_groups=mesh['tm'=16,'space'=16] {'tm'}, dimensions={1} | all-to-all | bytes 1048576 | tf_op jit(solution)/shard_map/all_to_all | solution.py:110
  64.5 3.1 collective-permute-start.4
  67.5 4.0 %collective-permute-start.3 = (f32[2,128,1,8,128]{4,3,1,2,0:T(8,128)S(1)}, f32[2,128,1,8,128]{4,3,1,2,0:T(8,128)S(1)}, u32[]{:S(2)}, u32[]{:S(2)}) collective-permute-start(f32[2,128,1,8,128]{4,3,1,2,0:T(8,128)S(1)} %constant_dynamic-update-slice_fusion.2), channel_id=1, source_target_pairs={{0,16},{16,32},{32,48},{48,64},{64,80},{80,96},{96,112},{112,128},... | collective-permute-start | bytes 3145736 | tf_op jit(solution)/shard_map/ppermute | solution.py:32
  71.5 17.9 %collective-permute-done.4 = f32[2,128,1,8,128]{4,3,1,2,0:T(8,128)S(1)} collective-permute-done((f32[2,128,1,8,128]{4,3,1,2,0:T(8,128)S(1)}, f32[2,128,1,8,128]{4,3,1,2,0:T(8,128)S(1)}, u32[]{:S(2)}, u32[]{:S(2)}) %collective-permute-start.4) | collective-permute-done | bytes 1048608 | tf_op jit(solution)/shard_map/ppermute | solution.py:34
  89.5 1.6 pad_maximum_fusion.49
  91.0 1.9 collective-permute-start.5
  93.0 5.7 %collective-permute-start.6 = (f32[2,128,3,1,128]{4,3,1,2,0:T(1,128)}, f32[2,128,3,1,128]{4,3,1,2,0:T(1,128)}, u32[]{:S(2)}, u32[]{:S(2)}) collective-permute-start(f32[2,128,3,1,128]{4,3,1,2,0:T(1,128)} %get-tuple-element.16), channel_id=1, source_target_pairs={{1,0},{2,1},{3,2},{4,3},{5,4},{6,5},{7,6},{8,7},{9,8},{10,9},{11,1... | collective-permute-start | bytes 1179656 | tf_op jit(solution)/shard_map/ppermute | solution.py:34
  99.9 2.1 collective-permute-done.5
  102.0 1.5 collective-permute-done.6
  103.4 11.3 %select_maximum_fusion.15 = f32[2,128,3,10,130]{4,3,1,2,0:T(8,128)S(1)} fusion(f32[2,128,3,1,128]{4,3,1,2,0:T(1,128)} %collective-permute-done.6, f32[2,128,3,1,128]{4,3,1,2,0:T(1,128)} %collective-permute-done.5, f32[2,128,1,8,128]{4,3,1,2,0:T(8,128)} %copy-done.7, f32[2,128,1,8,128]{4,3,1,2,0:T(8,128)} %copy-done.4, f32[2,128,1,8,128]{4,3,1,2,0:T(8,128)} %copy-done.9), kind=kLoop, calls=%fused_computation.18 | loop fusion | flops 11980800 | bytes 7925760 | tf_op jit(solution)/shard_map/concatenate | solution.py:30
  114.8 2.1 fusion.34
  117.3 3.6 %collective-permute-start.7 = (f32[2,128,1,8,128]{4,3,1,2,0:T(8,128)S(1)}, f32[2,128,1,8,128]{4,3,1,2,0:T(8,128)S(1)}, u32[]{:S(2)}, u32[]{:S(2)}) collective-permute-start(f32[2,128,1,8,128]{4,3,1,2,0:T(8,128)S(1)} %pad_maximum_fusion.30), channel_id=1, source_target_pairs={{0,16},{16,32},{32,48},{48,64},{64,80},{80,96},{96,112},{112,128},... | collective-permute-start | bytes 3145736 | tf_op jit(solution)/shard_map/ppermute | solution.py:32
  120.9 1.9 collective-permute-start.8
  122.9 9.8 %collective-permute-done.7 = f32[2,128,1,8,128]{4,3,1,2,0:T(8,128)S(1)} collective-permute-done((f32[2,128,1,8,128]{4,3,1,2,0:T(8,128)S(1)}, f32[2,128,1,8,128]{4,3,1,2,0:T(8,128)S(1)}, u32[]{:S(2)}, u32[]{:S(2)}) %collective-permute-start.7) | collective-permute-done | bytes 1048608 | tf_op jit(solution)/shard_map/ppermute | solution.py:32
  132.7 15.0 %collective-permute-done.8 = f32[2,128,1,8,128]{4,3,1,2,0:T(8,128)S(1)} collective-permute-done((f32[2,128,1,8,128]{4,3,1,2,0:T(8,128)S(1)}, f32[2,128,1,8,128]{4,3,1,2,0:T(8,128)S(1)}, u32[]{:S(2)}, u32[]{:S(2)}) %collective-permute-start.8) | collective-permute-done | bytes 1048608 | tf_op jit(solution)/shard_map/ppermute | solution.py:34
  148.3 1.9 collective-permute-start.9
  150.2 6.8 %collective-permute-start.10 = (f32[2,128,3,1,128]{4,3,1,2,0:T(1,128)S(1)}, f32[2,128,3,1,128]{4,3,1,2,0:T(1,128)S(1)}, u32[]{:S(2)}, u32[]{:S(2)}) collective-permute-start(f32[2,128,3,1,128]{4,3,1,2,0:T(1,128)S(1)} %get-tuple-element.14), channel_id=1, source_target_pairs={{1,0},{2,1},{3,2},{4,3},{5,4},{6,5},{7,6},{8,7},{9,8},{10,9},{11,1... | collective-permute-start | bytes 1179656 | tf_op jit(solution)/shard_map/ppermute | solution.py:34
  157.1 3.2 %collective-permute-done.9 = f32[2,128,3,1,128]{4,3,1,2,0:T(1,128)S(1)} collective-permute-done((f32[2,128,3,1,128]{4,3,1,2,0:T(1,128)S(1)}, f32[2,128,3,1,128]{4,3,1,2,0:T(1,128)S(1)}, u32[]{:S(2)}, u32[]{:S(2)}) %collective-permute-start.9) | collective-permute-done | bytes 393248 | tf_op jit(solution)/shard_map/ppermute | solution.py:32
  160.3 1.5 collective-permute-done.10
  161.8 10.6 %select_maximum_fusion.10 = f32[2,128,3,10,130]{4,3,1,2,0:T(8,128)S(1)} fusion(f32[2,128,3,1,128]{4,3,1,2,0:T(1,128)S(1)} %collective-permute-done.10, f32[2,128,3,1,128]{4,3,1,2,0:T(1,128)S(1)} %collective-permute-done.9, f32[2,128,1,8,128]{4,3,1,2,0:T(8,128)S(1)} %collective-permute-done.8, f32[2,128,1,8,128]{4,3,1,2,0:T(8,128)S(1)} %collective-permute-done.7, ...), kind=kLoop, calls=%fused_computation.13 | loop fusion | flops 13977600 | bytes 7925760 | tf_op jit(solution)/shard_map/concatenate | solution.py:30
  173.8 2.0 collective-permute-start.11
  175.8 2.4 collective-permute-start.12
  178.2 9.3 %collective-permute-done.11 = f32[2,128,1,8,128]{4,3,1,2,0:T(8,128)S(1)} collective-permute-done((f32[2,128,1,8,128]{4,3,1,2,0:T(8,128)S(1)}, f32[2,128,1,8,128]{4,3,1,2,0:T(8,128)S(1)}, u32[]{:S(2)}, u32[]{:S(2)}) %collective-permute-start.11) | collective-permute-done | bytes 1048608 | tf_op jit(solution)/shard_map/ppermute | solution.py:32
  187.6 15.5 %collective-permute-done.12 = f32[2,128,1,8,128]{4,3,1,2,0:T(8,128)S(1)} collective-permute-done((f32[2,128,1,8,128]{4,3,1,2,0:T(8,128)S(1)}, f32[2,128,1,8,128]{4,3,1,2,0:T(8,128)S(1)}, u32[]{:S(2)}, u32[]{:S(2)}) %collective-permute-start.12) | collective-permute-done | bytes 1048608 | tf_op jit(solution)/shard_map/ppermute | solution.py:34
  203.7 2.7 collective-permute-start.13
  206.4 6.3 %collective-permute-start.14 = (f32[2,128,3,1,128]{4,3,1,2,0:T(1,128)S(1)}, f32[2,128,3,1,128]{4,3,1,2,0:T(1,128)S(1)}, u32[]{:S(2)}, u32[]{:S(2)}) collective-permute-start(f32[2,128,3,1,128]{4,3,1,2,0:T(1,128)S(1)} %get-tuple-element.12), channel_id=1, source_target_pairs={{1,0},{2,1},{3,2},{4,3},{5,4},{6,5},{7,6},{8,7},{9,8},{10,9},{11,1... | collective-permute-start | bytes 1179656 | tf_op jit(solution)/shard_map/ppermute | solution.py:34
  212.7 3.0 collective-permute-done.13
  215.7 1.5 collective-permute-done.14
  217.2 10.6 %select_maximum_fusion.5 = f32[2,128,3,10,130]{4,3,1,2,0:T(8,128)S(1)} fusion(f32[2,128,3,1,128]{4,3,1,2,0:T(1,128)S(1)} %collective-permute-done.14, f32[2,128,3,1,128]{4,3,1,2,0:T(1,128)S(1)} %collective-permute-done.13, f32[2,128,1,8,128]{4,3,1,2,0:T(8,128)S(1)} %collective-permute-done.12, f32[2,128,1,8,128]{4,3,1,2,0:T(8,128)S(1)} %collective-permute-done.11, ...), kind=kLoop, calls=%fused_computation.8 | loop fusion | flops 13977600 | bytes 7925760 | tf_op jit(solution)/shard_map/concatenate | solution.py:30
  229.3 2.0 collective-permute-start.15
  231.3 2.4 collective-permute-start.16
  233.7 9.3 %collective-permute-done.15 = f32[2,128,1,8,128]{4,3,1,2,0:T(8,128)S(1)} collective-permute-done((f32[2,128,1,8,128]{4,3,1,2,0:T(8,128)S(1)}, f32[2,128,1,8,128]{4,3,1,2,0:T(8,128)S(1)}, u32[]{:S(2)}, u32[]{:S(2)}) %collective-permute-start.15) | collective-permute-done | bytes 1048608 | tf_op jit(solution)/shard_map/ppermute | solution.py:32
  243.0 14.3 %collective-permute-done.16 = f32[2,128,1,8,128]{4,3,1,2,0:T(8,128)S(1)} collective-permute-done((f32[2,128,1,8,128]{4,3,1,2,0:T(8,128)S(1)}, f32[2,128,1,8,128]{4,3,1,2,0:T(8,128)S(1)}, u32[]{:S(2)}, u32[]{:S(2)}) %collective-permute-start.16) | collective-permute-done | bytes 1048608 | tf_op jit(solution)/shard_map/ppermute | solution.py:34
  258.0 4.8 %collective-permute-start.17 = (f32[2,128,3,1,128]{4,3,1,2,0:T(1,128)S(1)}, f32[2,128,3,1,128]{4,3,1,2,0:T(1,128)S(1)}, u32[]{:S(2)}, u32[]{:S(2)}) collective-permute-start(f32[2,128,3,1,128]{4,3,1,2,0:T(1,128)S(1)} %get-tuple-element.9), channel_id=1, source_target_pairs={{0,1},{1,2},{2,3},{3,4},{4,5},{5,6},{6,7},{7,8},{8,9},{9,10},{10,1... | collective-permute-start | bytes 1179656 | tf_op jit(solution)/shard_map/ppermute | solution.py:32
  262.8 3.7 %collective-permute-start.18 = (f32[2,128,3,1,128]{4,3,1,2,0:T(1,128)S(1)}, f32[2,128,3,1,128]{4,3,1,2,0:T(1,128)S(1)}, u32[]{:S(2)}, u32[]{:S(2)}) collective-permute-start(f32[2,128,3,1,128]{4,3,1,2,0:T(1,128)S(1)} %get-tuple-element.10), channel_id=1, source_target_pairs={{1,0},{2,1},{3,2},{4,3},{5,4},{6,5},{7,6},{8,7},{9,8},{10,9},{11,1... | collective-permute-start | bytes 1179656 | tf_op jit(solution)/shard_map/ppermute | solution.py:34
  266.5 3.1 collective-permute-done.17
  269.6 8.4 %collective-permute-done.18 = f32[2,128,3,1,128]{4,3,1,2,0:T(1,128)S(1)} collective-permute-done((f32[2,128,3,1,128]{4,3,1,2,0:T(1,128)S(1)}, f32[2,128,3,1,128]{4,3,1,2,0:T(1,128)S(1)}, u32[]{:S(2)}, u32[]{:S(2)}) %collective-permute-start.18) | collective-permute-done | bytes 393248 | tf_op jit(solution)/shard_map/ppermute | solution.py:34
  278.0 10.6 %select_maximum_fusion = f32[2,128,3,10,130]{4,3,1,2,0:T(8,128)S(1)} fusion(f32[2,128,3,1,128]{4,3,1,2,0:T(1,128)S(1)} %collective-permute-done.18, f32[2,128,3,1,128]{4,3,1,2,0:T(1,128)S(1)} %collective-permute-done.17, f32[2,128,1,8,128]{4,3,1,2,0:T(8,128)S(1)} %collective-permute-done.16, f32[2,128,1,8,128]{4,3,1,2,0:T(8,128)S(1)} %collective-permute-done.15, ...), kind=kLoop, calls=%fused_computation.3 | loop fusion | flops 13977600 | bytes 7925760 | tf_op jit(solution)/shard_map/concatenate | solution.py:30
  292.8 7.0 %all-to-all-start.1 = ((f32[128,1,8,128]{3,2,1,0:T(8,128)}), f32[128,1,8,128]{3,2,1,0:T(8,128)S(1)}, u32[]{:S(2)}, u32[]{:S(2)}) async-start(f32[128,1,8,128]{3,2,1,0:T(8,128)} %bitcast.27), calls=%async_computation.1 | async-start | bytes 1048576 | tf_op jit(solution)/shard_map/all_to_all | solution.py:130
  299.8 11.3 %all-to-all-done.1 = f32[128,1,8,128]{3,2,1,0:T(8,128)S(1)} async-done(((f32[128,1,8,128]{3,2,1,0:T(8,128)}), f32[128,1,8,128]{3,2,1,0:T(8,128)S(1)}, u32[]{:S(2)}, u32[]{:S(2)}) %all-to-all-start.1) | async-done | bytes 524320 | tf_op jit(solution)/shard_map/all_to_all | solution.py:130
  (87 shorter events, 27.2 us)
Async XLA Ops:
  1.2 12.5 %collective-permute-start = (f32[1,16,8,128]{3,1,2,0:T(8,128)S(1)}, f32[1,16,8,128]{3,1,2,0:T(8,128)S(1)}, u32[]{:S(2)}, u32[]{:S(2)}) collective-permute-start(f32[1,16,8,128]{3,1,2,0:T(8,128)S(1)} %slice.335), channel_id=1, source_target_pairs={{16,0},{32,16},{48,32},{64,48},{80,64},{96,80},{112,96},{128,112},... | collective-permute-start | bytes 196616 | tf_op jit(solution)/shard_map/ppermute | solution.py:21
  13.7 1.1 copy-start.16
  13.7 1.0 copy-start.6
  14.8 22.2 %collective-permute-start.1 = (f32[14,16,1,128]{3,1,2,0:T(8,128)S(1)}, f32[14,16,1,128]{3,1,2,0:T(8,128)S(1)}, u32[]{:S(2)}, u32[]{:S(2)}) collective-permute-start(f32[14,16,1,128]{3,1,2,0:T(8,128)S(1)} %get-tuple-element.33), channel_id=1, source_target_pairs={{0,1},{1,2},{2,3},{3,4},{4,5},{5,6},{6,7},{7,8},{8,9},{9,10},{10,1... | collective-permute-start | bytes 344072 | tf_op jit(solution)/shard_map/ppermute | solution.py:32
  18.3 18.7 %collective-permute-start.2 = (f32[14,16,1,128]{3,1,2,0:T(8,128)S(1)}, f32[14,16,1,128]{3,1,2,0:T(8,128)}, u32[]{:S(2)}, u32[]{:S(2)}) collective-permute-start(f32[14,16,1,128]{3,1,2,0:T(8,128)S(1)} %get-tuple-element.34), channel_id=1, source_target_pairs={{1,0},{2,1},{3,2},{4,3},{5,4},{6,5},{7,6},{8,7},{9,8},{10,9},{11,1... | collective-permute-start | bytes 344072 | tf_op jit(solution)/shard_map/ppermute | solution.py:34
  62.4 1.0 copy-start.12
  63.3 26.2 %copy-start.14 = (f32[128,1024]{1,0:T(8,128)}, f32[128,1024]{1,0:T(8,128)S(1)}, u32[]{:S(2)}) copy-start(f32[128,1024]{1,0:T(8,128)S(1)} %fusion.50) | copy-start | bytes 1572868
  63.4 0.8 copy-start
  63.5 1.0 copy-start.2
  64.5 25.0 %copy-start.4 = (f32[2,128,1,8,128]{4,3,1,2,0:T(8,128)}, f32[2,128,1,8,128]{4,3,1,2,0:T(8,128)S(1)}, u32[]{:S(2)}) copy-start(f32[2,128,1,8,128]{4,3,1,2,0:T(8,128)S(1)} %constant_dynamic-update-slice_fusion.2) | copy-start | bytes 3145732
  64.5 25.0 %collective-permute-start.4 = (f32[2,128,1,8,128]{4,3,1,2,0:T(8,128)S(1)}, f32[2,128,1,8,128]{4,3,1,2,0:T(8,128)S(1)}, u32[]{:S(2)}, u32[]{:S(2)}) collective-permute-start(f32[2,128,1,8,128]{4,3,1,2,0:T(8,128)S(1)} %constant_dynamic-update-slice_fusion.2), channel_id=1, source_target_pairs={{16,0},{32,16},{48,32},{64,48},{80,64},{96,80},{112,96},{128,112},... | collective-permute-start | bytes 3145736 | tf_op jit(solution)/shard_map/ppermute | solution.py:34
  67.5 21.9 %collective-permute-start.3 = (f32[2,128,1,8,128]{4,3,1,2,0:T(8,128)S(1)}, f32[2,128,1,8,128]{4,3,1,2,0:T(8,128)S(1)}, u32[]{:S(2)}, u32[]{:S(2)}) collective-permute-start(f32[2,128,1,8,128]{4,3,1,2,0:T(8,128)S(1)} %constant_dynamic-update-slice_fusion.2), channel_id=1, source_target_pairs={{0,16},{16,32},{32,48},{48,64},{64,80},{80,96},{96,112},{112,128},... | collective-permute-start | bytes 3145736 | tf_op jit(solution)/shard_map/ppermute | solution.py:32
  89.4 1.6 copy-start.7
  89.5 1.6 copy-start.9
  91.0 10.9 %collective-permute-start.5 = (f32[2,128,3,1,128]{4,3,1,2,0:T(1,128)}, f32[2,128,3,1,128]{4,3,1,2,0:T(1,128)}, u32[]{:S(2)}, u32[]{:S(2)}) collective-permute-start(f32[2,128,3,1,128]{4,3,1,2,0:T(1,128)} %get-tuple-element.15), channel_id=1, source_target_pairs={{0,1},{1,2},{2,3},{3,4},{4,5},{5,6},{6,7},{7,8},{8,9},{9,10},{10,1... | collective-permute-start | bytes 1179656 | tf_op jit(solution)/shard_map/ppermute | solution.py:32
  93.0 10.5 %collective-permute-start.6 = (f32[2,128,3,1,128]{4,3,1,2,0:T(1,128)}, f32[2,128,3,1,128]{4,3,1,2,0:T(1,128)}, u32[]{:S(2)}, u32[]{:S(2)}) collective-permute-start(f32[2,128,3,1,128]{4,3,1,2,0:T(1,128)} %get-tuple-element.16), channel_id=1, source_target_pairs={{1,0},{2,1},{3,2},{4,3},{5,4},{6,5},{7,6},{8,7},{9,8},{10,9},{11,1... | collective-permute-start | bytes 1179656 | tf_op jit(solution)/shard_map/ppermute | solution.py:34
  98.6 16.1 %copy-start.5 = (f32[2,128,1,8,128]{4,3,1,2,0:T(8,128)S(1)}, f32[2,128,1,8,128]{4,3,1,2,0:T(8,128)}, u32[]{:S(2)}) copy-start(f32[2,128,1,8,128]{4,3,1,2,0:T(8,128)} %copy-done.4) | copy-start | bytes 3145732
  98.6 16.1 %copy-start.8 = (f32[2,128,1,8,128]{4,3,1,2,0:T(8,128)S(1)}, f32[2,128,1,8,128]{4,3,1,2,0:T(8,128)}, u32[]{:S(2)}) copy-start(f32[2,128,1,8,128]{4,3,1,2,0:T(8,128)} %copy-done.7) | copy-start | bytes 3145732
  98.6 16.1 %copy-start.10 = (f32[2,128,1,8,128]{4,3,1,2,0:T(8,128)S(1)}, f32[2,128,1,8,128]{4,3,1,2,0:T(8,128)}, u32[]{:S(2)}) copy-start(f32[2,128,1,8,128]{4,3,1,2,0:T(8,128)} %copy-done.9) | copy-start | bytes 3145732
  99.7 17.1 %copy-start.1 = (f32[16,8,8,128]{3,2,1,0:T(8,128)S(1)}, f32[16,8,8,128]{3,2,1,0:T(8,128)}, u32[]{:S(2)}) copy-start(f32[16,8,8,128]{3,2,1,0:T(8,128)} %copy-done) | copy-start | bytes 1572868
  99.7 17.1 %copy-start.3 = (f32[16,8,8,128]{3,2,1,0:T(8,128)S(1)}, f32[16,8,8,128]{3,2,1,0:T(8,128)}, u32[]{:S(2)}) copy-start(f32[16,8,8,128]{3,2,1,0:T(8,128)} %copy-done.2) | copy-start | bytes 1572868
  117.3 15.4 %collective-permute-start.7 = (f32[2,128,1,8,128]{4,3,1,2,0:T(8,128)S(1)}, f32[2,128,1,8,128]{4,3,1,2,0:T(8,128)S(1)}, u32[]{:S(2)}, u32[]{:S(2)}) collective-permute-start(f32[2,128,1,8,128]{4,3,1,2,0:T(8,128)S(1)} %pad_maximum_fusion.30), channel_id=1, source_target_pairs={{0,16},{16,32},{32,48},{48,64},{64,80},{80,96},{96,112},{112,128},... | collective-permute-start | bytes 3145736 | tf_op jit(solution)/shard_map/ppermute | solution.py:32
  120.9 26.7 %collective-permute-start.8 = (f32[2,128,1,8,128]{4,3,1,2,0:T(8,128)S(1)}, f32[2,128,1,8,128]{4,3,1,2,0:T(8,128)S(1)}, u32[]{:S(2)}, u32[]{:S(2)}) collective-permute-start(f32[2,128,1,8,128]{4,3,1,2,0:T(8,128)S(1)} %pad_maximum_fusion.30), channel_id=1, source_target_pairs={{16,0},{32,16},{48,32},{64,48},{80,64},{96,80},{112,96},{128,112},... | collective-permute-start | bytes 3145736 | tf_op jit(solution)/shard_map/ppermute | solution.py:34
  148.3 12.0 %collective-permute-start.9 = (f32[2,128,3,1,128]{4,3,1,2,0:T(1,128)S(1)}, f32[2,128,3,1,128]{4,3,1,2,0:T(1,128)S(1)}, u32[]{:S(2)}, u32[]{:S(2)}) collective-permute-start(f32[2,128,3,1,128]{4,3,1,2,0:T(1,128)S(1)} %get-tuple-element.13), channel_id=1, source_target_pairs={{0,1},{1,2},{2,3},{3,4},{4,5},{5,6},{6,7},{7,8},{8,9},{9,10},{10,1... | collective-permute-start | bytes 1179656 | tf_op jit(solution)/shard_map/ppermute | solution.py:32
  150.2 11.5 %collective-permute-start.10 = (f32[2,128,3,1,128]{4,3,1,2,0:T(1,128)S(1)}, f32[2,128,3,1,128]{4,3,1,2,0:T(1,128)S(1)}, u32[]{:S(2)}, u32[]{:S(2)}) collective-permute-start(f32[2,128,3,1,128]{4,3,1,2,0:T(1,128)S(1)} %get-tuple-element.14), channel_id=1, source_target_pairs={{1,0},{2,1},{3,2},{4,3},{5,4},{6,5},{7,6},{8,7},{9,8},{10,9},{11,1... | collective-permute-start | bytes 1179656 | tf_op jit(solution)/shard_map/ppermute | solution.py:34
  173.8 13.7 %collective-permute-start.11 = (f32[2,128,1,8,128]{4,3,1,2,0:T(8,128)S(1)}, f32[2,128,1,8,128]{4,3,1,2,0:T(8,128)S(1)}, u32[]{:S(2)}, u32[]{:S(2)}) collective-permute-start(f32[2,128,1,8,128]{4,3,1,2,0:T(8,128)S(1)} %pad_maximum_fusion.31), channel_id=1, source_target_pairs={{0,16},{16,32},{32,48},{48,64},{64,80},{80,96},{96,112},{112,128},... | collective-permute-start | bytes 3145736 | tf_op jit(solution)/shard_map/ppermute | solution.py:32
  175.8 27.3 %collective-permute-start.12 = (f32[2,128,1,8,128]{4,3,1,2,0:T(8,128)S(1)}, f32[2,128,1,8,128]{4,3,1,2,0:T(8,128)S(1)}, u32[]{:S(2)}, u32[]{:S(2)}) collective-permute-start(f32[2,128,1,8,128]{4,3,1,2,0:T(8,128)S(1)} %pad_maximum_fusion.31), channel_id=1, source_target_pairs={{16,0},{32,16},{48,32},{64,48},{80,64},{96,80},{112,96},{128,112},... | collective-permute-start | bytes 3145736 | tf_op jit(solution)/shard_map/ppermute | solution.py:34
  203.7 12.0 %collective-permute-start.13 = (f32[2,128,3,1,128]{4,3,1,2,0:T(1,128)S(1)}, f32[2,128,3,1,128]{4,3,1,2,0:T(1,128)S(1)}, u32[]{:S(2)}, u32[]{:S(2)}) collective-permute-start(f32[2,128,3,1,128]{4,3,1,2,0:T(1,128)S(1)} %get-tuple-element.11), channel_id=1, source_target_pairs={{0,1},{1,2},{2,3},{3,4},{4,5},{5,6},{6,7},{7,8},{8,9},{9,10},{10,1... | collective-permute-start | bytes 1179656 | tf_op jit(solution)/shard_map/ppermute | solution.py:32
  206.4 10.8 %collective-permute-start.14 = (f32[2,128,3,1,128]{4,3,1,2,0:T(1,128)S(1)}, f32[2,128,3,1,128]{4,3,1,2,0:T(1,128)S(1)}, u32[]{:S(2)}, u32[]{:S(2)}) collective-permute-start(f32[2,128,3,1,128]{4,3,1,2,0:T(1,128)S(1)} %get-tuple-element.12), channel_id=1, source_target_pairs={{1,0},{2,1},{3,2},{4,3},{5,4},{6,5},{7,6},{8,7},{9,8},{10,9},{11,1... | collective-permute-start | bytes 1179656 | tf_op jit(solution)/shard_map/ppermute | solution.py:34
  229.3 13.7 %collective-permute-start.15 = (f32[2,128,1,8,128]{4,3,1,2,0:T(8,128)S(1)}, f32[2,128,1,8,128]{4,3,1,2,0:T(8,128)S(1)}, u32[]{:S(2)}, u32[]{:S(2)}) collective-permute-start(f32[2,128,1,8,128]{4,3,1,2,0:T(8,128)S(1)} %pad_maximum_fusion.32), channel_id=1, source_target_pairs={{0,16},{16,32},{32,48},{48,64},{64,80},{80,96},{96,112},{112,128},... | collective-permute-start | bytes 3145736 | tf_op jit(solution)/shard_map/ppermute | solution.py:32
  231.3 26.0 %collective-permute-start.16 = (f32[2,128,1,8,128]{4,3,1,2,0:T(8,128)S(1)}, f32[2,128,1,8,128]{4,3,1,2,0:T(8,128)S(1)}, u32[]{:S(2)}, u32[]{:S(2)}) collective-permute-start(f32[2,128,1,8,128]{4,3,1,2,0:T(8,128)S(1)} %pad_maximum_fusion.32), channel_id=1, source_target_pairs={{16,0},{32,16},{48,32},{64,48},{80,64},{96,80},{112,96},{128,112},... | collective-permute-start | bytes 3145736 | tf_op jit(solution)/shard_map/ppermute | solution.py:34
  258.0 11.6 %collective-permute-start.17 = (f32[2,128,3,1,128]{4,3,1,2,0:T(1,128)S(1)}, f32[2,128,3,1,128]{4,3,1,2,0:T(1,128)S(1)}, u32[]{:S(2)}, u32[]{:S(2)}) collective-permute-start(f32[2,128,3,1,128]{4,3,1,2,0:T(1,128)S(1)} %get-tuple-element.9), channel_id=1, source_target_pairs={{0,1},{1,2},{2,3},{3,4},{4,5},{5,6},{6,7},{7,8},{8,9},{9,10},{10,1... | collective-permute-start | bytes 1179656 | tf_op jit(solution)/shard_map/ppermute | solution.py:32
  262.7 27.0 %copy-start.15 = (f32[128,1024]{1,0:T(8,128)S(1)}, f32[128,1024]{1,0:T(8,128)}, u32[]{:S(2)}) copy-start(f32[128,1024]{1,0:T(8,128)} %copy-done.14) | copy-start | bytes 1572868
  262.7 28.1 %copy-start.13 = (f32[128,1024]{1,0:T(8,128)S(1)}, f32[128,1024]{1,0:T(8,128)}, u32[]{:S(2)}) copy-start(f32[128,1024]{1,0:T(8,128)} %copy-done.12) | copy-start | bytes 1572868
  262.8 48.3 %copy-start.11 = (f32[8,16,8,128]{3,2,1,0:T(8,128)S(1)}, f32[8,16,8,128]{3,2,1,0:T(8,128)}, u32[]{:S(2)}) copy-start(f32[8,16,8,128]{3,2,1,0:T(8,128)} %param.7) | copy-start | bytes 1572868
  262.8 15.2 %collective-permute-start.18 = (f32[2,128,3,1,128]{4,3,1,2,0:T(1,128)S(1)}, f32[2,128,3,1,128]{4,3,1,2,0:T(1,128)S(1)}, u32[]{:S(2)}, u32[]{:S(2)}) collective-permute-start(f32[2,128,3,1,128]{4,3,1,2,0:T(1,128)S(1)} %get-tuple-element.10), channel_id=1, source_target_pairs={{1,0},{2,1},{3,2},{4,3},{5,4},{6,5},{7,6},{8,7},{9,8},{10,9},{11,1... | collective-permute-start | bytes 1179656 | tf_op jit(solution)/shard_map/ppermute | solution.py:34
  292.8 18.3 %all-to-all-start.1 = ((f32[128,1,8,128]{3,2,1,0:T(8,128)}), f32[128,1,8,128]{3,2,1,0:T(8,128)S(1)}, u32[]{:S(2)}, u32[]{:S(2)}) async-start(f32[128,1,8,128]{3,2,1,0:T(8,128)} %bitcast.27), calls=%async_computation.1 | async-start | bytes 1048576 | tf_op jit(solution)/shard_map/all_to_all | solution.py:130
where the time goes:
time: 314 us; the launch traced here: 312 us
  waiting for transfers between devices  127 us (40%)
  other arithmetic  74.7 us (24%)
  starting transfers between devices  74.1 us (24%)
  blocking collectives  18.3 us (6%)
  local copies, waits for them, and re-layouts  13.6 us (4%)
  matrix products  3.91 us (1%)
    ppermute x9, waiting for transfers between devices, with_halo(): lax.ppermute(head, axis, [((i + 1) % count, i) for i in range(ends)])  75.6 us
    concatenate x5, other arithmetic, with_halo(): jnp.concatenate([lax.ppermute(tail, axis, [(i, (i + 1) % count) for i in...  45.7 us
    ppermute x9, waiting for transfers between devices, with_halo(): lax.ppermute(tail, axis, [(i, (i + 1) % count) for i in range(ends)])  39.8 us
    ppermute x9, starting transfers between devices, with_halo(): lax.ppermute(head, axis, [((i + 1) % count, i) for i in range(ends)])  38.1 us
    ppermute x9, starting transfers between devices, with_halo(): lax.ppermute(tail, axis, [(i, (i + 1) % count) for i in range(ends)])  26.4 us
    all_to_all x1, blocking collectives, body(): lax.all_to_all(scaled, 'tm', split_axis=1, concat_axis=0, tiled=True)  18.3 us
    unnamed x8, other arithmetic  13.3 us
    all_to_all x1, waiting for transfers between devices, body(): lax.all_to_all(restored, 'tm', split_axis=0, concat_axis=1, tiled=True)  11.3 us
  transfers between devices with their start and end apart: 20, of which 16 were waited for; matrix products, arithmetic and copies ran while one was open for 8% of the time, Pallas kernels for 0%

commit v1 on v0

v1 whole, which is shorter than its diff:
```python
import functools

import jax
import jax.numpy as jnp
from jax import lax
from jax.experimental import pallas as pl
from jax.experimental.pallas import tpu as pltpu
from jax.sharding import PartitionSpec as P

MESH = pl.DeviceIdType.MESH

LEV = 16
TX = 8
NY = 128
STEPS_DEV = 8
DEPTH = 5
CIRC_ALPHA = 0.1

RATES, INNOV, CELLS, STATE, INNOV_UP, CELLS_UP, PER_SIDE = 0, 4, 5, 6, 14, 15, 16
INNOV_T, CELLS_T, STATE_T = 2 * PER_SIDE, 2 * PER_SIDE + 1, 2 * PER_SIDE + 2
TRANSFERS = STATE_T + DEPTH


def fill_forcing(forcing, which, plane, parts):
    x_of = lax.broadcasted_iota(jnp.int32, (TX, NY), 0)
    y_of = lax.broadcasted_iota(jnp.int32, (NY, NY), 0)
    total = None
    for values, cells, low, high in parts:
        column = cells // NY
        row = cells % NY
        mask = (column == x_of) & (x_of >= low) & (x_of < high)
        head = values.astype(jnp.bfloat16).astype(jnp.float32)
        rest = values - head
        pieces = [
            jnp.where(mask[None], piece[:, None, :], 0.0).reshape(LEV * TX, NY).astype(jnp.bfloat16)
            for piece in (head, rest)
        ]
        hot = jnp.where(row == y_of, 1.0, 0.0).astype(jnp.bfloat16)
        part = lax.dot_general(
            jnp.concatenate(pieces, axis=1),
            jnp.concatenate([hot, hot], axis=1),
            (((1,), (1,)), ((), ())),
            preferred_element_type=jnp.float32,
        )
        total = part if total is None else total + part
    forcing[plane, :, which] = total.reshape(LEV, TX, NY)


def kernel(
    time_parts, tiles,
    a, innov, cells, dif, wx, wy, vm, out,
    ac, hl, hr, a8, nc, nl, nr, kc, kl, kr, kc2, kl2, kr2, rc, rl, rr, coef, forcing, va, vb, ob,
    send, recv, local,
):
    t = lax.axis_index("tm")
    s = lax.axis_index("space")
    before = lax.rem(t + time_parts - 1, time_parts)
    after = lax.rem(t + 1, time_parts)
    has_left = s > 0
    has_right = s < tiles - 1
    is_last = t == time_parts - 1

    barrier = pltpu.get_barrier_semaphore()
    pl.semaphore_signal(barrier, inc=1, device_id=(after, s), device_id_type=MESH)

    @pl.when(has_left)
    def _():
        pl.semaphore_signal(barrier, inc=1, device_id=(t, s - 1), device_id_type=MESH)
        pl.semaphore_signal(barrier, inc=1, device_id=(after, s - 1), device_id_type=MESH)

    @pl.when(has_right)
    def _():
        pl.semaphore_signal(barrier, inc=1, device_id=(t, s + 1), device_id_type=MESH)
        pl.semaphore_signal(barrier, inc=1, device_id=(after, s + 1), device_id_type=MESH)

    fields = (dif, wx, wy, vm)
    loads = [
        pltpu.make_async_copy(innov, nc.at[pl.ds(0, STEPS_DEV)], local.at[0]),
        pltpu.make_async_copy(cells, kc, local.at[1]),
        pltpu.make_async_copy(a.at[pl.ds(DEPTH, 3)], ac.at[pl.ds(0, 3)], local.at[2]),
    ] + [pltpu.make_async_copy(f, rc.at[i], local.at[3 + i]) for i, f in enumerate(fields)]
    for load in loads:
        load.start()

    def remote(number, src, dst, device):
        return pltpu.make_async_remote_copy(
            src_ref=src, dst_ref=dst, send_sem=send.at[number], recv_sem=recv.at[number],
            device_id=device, device_id_type=MESH,
        )

    def side(base, step, first, width, halo, inn, cel, cel_up, rat):
        here, up = (t, s + step), (before, s + step)
        cols = pl.ds(first, width)
        edge = pl.ds(4, 4) if step > 0 else pl.ds(0, 4)
        rates = [
            remote(base + RATES + i, f.at[:, cols if i < 2 else edge], rat.at[i, :, cols if i < 2 else edge], here)
            for i, f in enumerate(fields)
        ]
        early = [
            remote(base + CELLS, cells, cel, here),
            remote(base + INNOV, innov, inn.at[pl.ds(0, STEPS_DEV)], here),
            remote(base + CELLS_UP, cells, cel_up, up),
            remote(base + INNOV_UP, innov.at[pl.ds(0, 4)], inn.at[pl.ds(STEPS_DEV, 4)], up),
        ]
        state = [
            remote(base + STATE + i, a.at[(i + DEPTH) % 8, :, cols], halo.at[i, :, cols], here if i < 3 else up)
            for i in range(8)
        ]
        return rates, early, state

    sides = (
        (has_right, has_left, side(0, 1, 3, 5, hl, nl, kl, kl2, rl)),
        (has_left, has_right, side(PER_SIDE, -1, 0, 5, hr, nr, kr, kr2, rr)),
    )
    up_early = [
        remote(CELLS_T, cells, kc2, (before, s)),
        remote(INNOV_T, innov.at[pl.ds(0, 4)], nc.at[pl.ds(STEPS_DEV, 4)], (before, s)),
    ]
    up_state = [remote(STATE_T + i, a.at[i], ac.at[3 + i], (before, s)) for i in range(DEPTH)]

    for has, (halo, inn, cel, cel_up, rat) in (
        (has_left, (hl, nl, kl, kl2, rl)),
        (has_right, (hr, nr, kr, kr2, rr)),
    ):

        @pl.when(jnp.logical_not(has))
        def _(refs=(halo, inn, cel, cel_up, rat)):
            for ref in refs:
                ref[...] = jnp.zeros_like(ref)

    neighbours = 1 + 2 * has_left.astype(jnp.int32) + 2 * has_right.astype(jnp.int32)
    pl.semaphore_wait(barrier, neighbours)
    for part in range(3):
        for sends, _, groups in sides:

            @pl.when(sends)
            def _(copies=groups[part]):
                for copy in copies:
                    copy.start()

        for copy in ([], up_early, up_state)[part]:
            copy.start()

    for load in loads:
        load.wait()

    def own_forcing(n, carry):
        fill_forcing(forcing, 0, n, [(nc[n], kc[pl.ds(n, 1)], 0, TX)])
        return carry

    lax.fori_loop(0, STEPS_DEV, own_forcing, 0)

    for _, receives, (rates, early, _) in sides:

        @pl.when(receives)
        def _(copies=rates + early):
            for copy in copies:
                copy.wait_recv()

    for copy in up_early:
        copy.wait_recv()

    x_of = lax.broadcasted_iota(jnp.int32, (TX, NY), 0)
    y_of = lax.broadcasted_iota(jnp.int32, (TX, NY), 1)
    first_half = x_of < 4
    is_first, is_end = x_of == 0, x_of == TX - 1

    def down_x(v):
        return pltpu.roll(v, 1, 0)

    def up_x(v):
        return pltpu.roll(v, TX - 1, 0)

    def make_rates(l, carry):
        def own(part):
            return part[0, l], part[1, l], part[2, l], part[3, l]

        dc, xc, yc, mc = own(rc)
        dl, xl, yl, ml = own(rl)
        dr, xr, yr, mr = own(rr)
        east_c, west_c = dc + jnp.maximum(-xc, 0.0), dc + jnp.maximum(xc, 0.0)
        east_l, west_l = dl + jnp.maximum(-xl, 0.0), dl + jnp.maximum(xl, 0.0)
        east_r, west_r = dr + jnp.maximum(-xr, 0.0), dr + jnp.maximum(xr, 0.0)
        dh = jnp.where(first_half, dr, dl)
        yh = jnp.where(first_half, yr, yl)
        mh = jnp.where(first_half, mr, ml)
        east_h = jnp.where(first_half, east_r, east_l)
        west_h = jnp.where(first_half, west_r, west_l)
        from_west = (
            jnp.where(is_first, down_x(east_l), down_x(east_c)),
            jnp.where(first_half, jnp.where(is_first, down_x(east_c), down_x(east_r)), down_x(east_l)),
        )
        from_east = (
            jnp.where(is_end, up_x(west_r), up_x(west_c)),
            jnp.where(first_half, up_x(west_r), jnp.where(is_end, up_x(west_c), up_x(west_l))),
        )
        for which, (d, e, w, y, m) in enumerate(
            ((dc, east_c, west_c, yc, mc), (dh, east_h, west_h, yh, mh))
        ):
            north, south = d + jnp.maximum(-y, 0.0), d + jnp.maximum(y, 0.0)
            coef[l, which, 0] = 1.0 - (e + w + north + south + m + m)
            coef[l, which, 1] = from_west[which]
            coef[l, which, 2] = from_east[which]
            coef[l, which, 3] = jnp.where(y_of == 0, 0.0, pltpu.roll(north, 1, 1))
            coef[l, which, 4] = jnp.where(y_of == NY - 1, 0.0, pltpu.roll(south, NY - 1, 1))
            coef[l, which, 5] = m
        return carry

    lax.fori_loop(0, LEV, make_rates, 0)

    def halo_forcing(n, carry):
        fill_forcing(forcing, 1, n, [(nl[n], kl[pl.ds(n, 1)], 4, TX), (nr[n], kr[pl.ds(n, 1)], 0, 4)])
        return carry

    lax.fori_loop(1, STEPS_DEV, halo_forcing, 0)

    def next_forcing(n, carry):
        m = n + STEPS_DEV
        fill_forcing(forcing, 0, m, [(nc[m], kc2[pl.ds(n, 1)], 0, TX)])
        fill_forcing(forcing, 1, m, [(nl[m], kl2[pl.ds(n, 1)], 4, TX), (nr[m], kr2[pl.ds(n, 1)], 0, 4)])
        return carry

    lax.fori_loop(0, 4, next_forcing, 0)

    def spread(l, which, v, west, east, force):
        total = force + coef[l, which, 0] * v
        total = total + coef[l, which, 1] * west
        total = total + coef[l, which, 2] * east
        total = total + coef[l, which, 3] * pltpu.roll(v, 1, 1)
        return total + coef[l, which, 4] * pltpu.roll(v, NY - 1, 1)

    def sweep(i, src, dst, plane, last):
        for l in range(LEV):
            c, h = src(l)
            cd, cu = down_x(c), up_x(c)
            if isinstance(h, tuple):
                left, right = h
                ld, rd, lu, ru = down_x(left), down_x(right), up_x(left), up_x(right)
                h = jnp.where(first_half, right, left)
                hd = jnp.where(first_half, rd, ld)
                hu = jnp.where(first_half, ru, lu)
                west_c, east_c = jnp.where(is_first, ld, cd), jnp.where(is_end, ru, cu)
            else:
                hd, hu = down_x(h), up_x(h)
                west_c, east_c = jnp.where(is_first, hd, cd), jnp.where(is_end, hu, cu)
            west_h, east_h = jnp.where(is_first, cd, hd), jnp.where(is_end, cu, hu)
            for which, (v, west, east) in enumerate(((c, west_c, east_c), (h, west_h, east_h))):
                if last and which:
                    continue
                total = spread(l, which, v, west, east, forcing[plane, l, which])
                for k in (l - 1, l + 1):
                    if 0 <= k < LEV:
                        o = src(k)[which]
                        if isinstance(o, tuple):
                            o = jnp.where(first_half, o[1], o[0])
                        total = total + coef[k, which, 5] * o
                if last:
                    ob[i, l] = total
                else:
                    dst[l, which] = total

    def chain(i, carry):
        for _, receives, (_, _, state) in sides:

            @pl.when(receives)
            def _(state=state):
                for k in range(8):

                    @pl.when(i == k)
                    def _(copy=state[k]):
                        copy.wait_recv()

        for k in range(DEPTH):

            @pl.when(i == k + 3)
            def _(copy=up_state[k]):
                copy.wait_recv()

        @pl.when(is_last & (i == 3))
        def _():
            a8[:, 0] = ac[3]
            for l in range(LEV):
                a8[l, 1] = jnp.where(first_half, hr[3, l], hl[3, l])
            for ref in (ac, hl, hr):
                ref[3] = jnp.zeros((LEV, TX, NY), jnp.float32)

        sweep(i, lambda l: (ac[i, l], (hl[i, l], hr[i, l])), va, i + 4, False)
        bufs = (va, vb)
        for k in range(2, DEPTH + 1):
            src, dst = bufs[k % 2], bufs[(k + 1) % 2]

            @pl.when(is_last & (i == k + 2))
            def _(src=src):
                src[...] = CIRC_ALPHA * (src[...] - a8[...])

            sweep(i, lambda l, src=src: (src[l, 0], src[l, 1]), dst, i + DEPTH - k, k == DEPTH)
        pltpu.make_async_copy(ob.at[i], out.at[i], local.at[7 + i]).start()
        return carry

    lax.fori_loop(0, STEPS_DEV, chain, 0)

    for i in range(STEPS_DEV):
        pltpu.make_async_copy(ob.at[i], out.at[i], local.at[7 + i]).wait()
    for sends, _, groups in sides:

        @pl.when(sends)
        def _(copies=groups[0] + groups[1] + groups[2]):
            for copy in copies:
                copy.wait_send()

    for copy in up_early + up_state:
        copy.wait_send()


def body(adjoint_iterate, innovations, station_cells, diffusivity, wind_x, wind_y, vertical_mixing):
    field = (LEV, TX, NY)
    f32, i32 = jnp.float32, jnp.int32
    scratch = (
        [pltpu.VMEM((STEPS_DEV,) + field, f32)] * 3
        + [pltpu.VMEM((LEV, 2, TX, NY), f32)]
        + [pltpu.VMEM((STEPS_DEV + 4, LEV, NY), f32)] * 3
        + [pltpu.VMEM((STEPS_DEV, NY), i32)] * 6
        + [pltpu.VMEM((4,) + field, f32)] * 3
        + [pltpu.VMEM((LEV, 2, 6, TX, NY), f32)]
        + [pltpu.VMEM((STEPS_DEV + 4, LEV, 2, TX, NY), f32)]
        + [pltpu.VMEM((LEV, 2, TX, NY), f32)] * 2
        + [pltpu.VMEM((STEPS_DEV,) + field, f32)]
        + [pltpu.SemaphoreType.DMA((TRANSFERS,))] * 2
        + [pltpu.SemaphoreType.DMA((7 + STEPS_DEV,))]
    )
    return pl.pallas_call(
        functools.partial(kernel, lax.axis_size("tm"), lax.axis_size("space")),
        out_shape=jax.ShapeDtypeStruct((STEPS_DEV,) + field, f32),
        in_specs=[pl.BlockSpec(memory_space=pl.ANY)] * 7,
        out_specs=pl.BlockSpec(memory_space=pl.ANY),
        scratch_shapes=scratch,
        compiler_params=pltpu.CompilerParams(
            collective_id=0, has_side_effects=True, vmem_limit_bytes=24 * 2**20
        ),
        name="update",
    )(adjoint_iterate, innovations, station_cells, diffusivity, wind_x, wind_y, vertical_mixing)


def solution(mesh):
    in_specs = (
        P("tm", None, "space", None),
        P("tm", None, "space"),
        P("tm", "space"),
        P(None, "space", None),
        P(None, "space", None),
        P(None, "space", None),
        P(None, "space", None),
    )
    out_specs = P("tm", None, "space", None)
    return jax.shard_map(body, mesh=mesh, in_specs=in_specs, out_specs=out_specs, check_vma=False)
```

time: 314 us -> 38.4 us (0.12)
  the two profiles are of different devices: /device:TPU:3 before, /device:TPU:29 now
where the time goes in v1:
time: 38.4 us; the launch traced here: 38.1 us
  Pallas kernels  31.3 us (82%)
  local copies, waits for them, and re-layouts  6.72 us (18%)
    pallas_call x1, Pallas kernels, body(): pl.pallas_call(functools.partial(kernel, lax.axis_size('tm'), lax.axis_si...  31.3 us
    unnamed x15, local copies, waits for them, and re-layouts  6.72 us

profile of v1, /device:TPU:29, one launch (start us, length us, event | category | flops | bytes accessed | tf_op | source)
XLA Modules:
  0.0 38.1 jit_solution(8834512037838685244)
XLA Ops:
  0.0 0.0 copy-start
  0.0 1.0 %copy-done = f32[8,16,8,128]{3,2,1,0:T(8,128)S(1)} copy-done((f32[8,16,8,128]{3,2,1,0:T(8,128)S(1)}, f32[8,16,8,128]{3,2,1,0:T(8,128)}, u32[]{:S(2)}) %copy-start) | copy-done | bytes 524312
  1.0 0.0 copy-start.1
  1.0 0.8 %copy-done.1 = f32[8,16,128]{2,1,0:T(8,128)S(1)} copy-done((f32[8,16,128]{2,1,0:T(8,128)S(1)}, f32[8,16,128]{2,1,0:T(8,128)}, u32[]{:S(2)}) %copy-start.1) | copy-done | bytes 65560
  1.9 0.0 copy-start.2
  1.9 0.8 %copy-done.2 = f32[16,8,128]{2,1,0:T(8,128)S(1)} copy-done((f32[16,8,128]{2,1,0:T(8,128)S(1)}, f32[16,8,128]{2,1,0:T(8,128)}, u32[]{:S(2)}) %copy-start.2) | copy-done | bytes 65560
  2.7 0.0 copy-start.3
  2.7 0.8 %copy-done.3 = f32[16,8,128]{2,1,0:T(8,128)S(1)} copy-done((f32[16,8,128]{2,1,0:T(8,128)S(1)}, f32[16,8,128]{2,1,0:T(8,128)}, u32[]{:S(2)}) %copy-start.3) | copy-done | bytes 65560
  3.6 0.0 copy-start.4
  3.6 0.8 %copy-done.4 = f32[16,8,128]{2,1,0:T(8,128)S(1)} copy-done((f32[16,8,128]{2,1,0:T(8,128)S(1)}, f32[16,8,128]{2,1,0:T(8,128)}, u32[]{:S(2)}) %copy-start.4) | copy-done | bytes 65560
  4.4 0.0 copy-start.5
  4.4 0.8 %copy-done.5 = f32[16,8,128]{2,1,0:T(8,128)S(1)} copy-done((f32[16,8,128]{2,1,0:T(8,128)S(1)}, f32[16,8,128]{2,1,0:T(8,128)}, u32[]{:S(2)}) %copy-start.5) | copy-done | bytes 65560
  5.2 0.0 copy-start.6
  5.2 0.7 %copy-done.6 = s32[8,128]{1,0:T(8,128)S(1)} copy-done((s32[8,128]{1,0:T(8,128)S(1)}, s32[8,128]{1,0:T(8,128)}, u32[]{:S(2)}) %copy-start.6) | copy-done | bytes 4120
  5.9 31.3 %update.1 = f32[8,16,8,128]{3,2,1,0:T(8,128)S(1)} custom-call(f32[8,16,8,128]{3,2,1,0:T(8,128)S(1)} %copy-done, f32[8,16,128]{2,1,0:T(8,128)S(1)} %copy-done.1, s32[8,128]{1,0:T(8,128)S(1)} %copy-done.6, f32[16,8,128]{2,1,0:T(8,128)S(1)} %copy-done.2, f32[16,8,128]{2,1,0:T(8,128)S(1)} %copy-done.3, f32[16,8,128]{2,1,0:T(8,128)S(1)} %copy-done.4, ...), custom_call_target="tpu_custom_call" | custom-call | tf_op jit(solution)/shard_map/update/pallas_call | solution.py:331
  37.3 0.8 %copy.9 = f32[8,16,8,128]{3,2,1,0:T(8,128)} copy(f32[8,16,8,128]{3,2,1,0:T(8,128)S(1)} %update.1) | data formatting | bytes 1048576
Async XLA Ops:
  0.0 1.0 %copy-start = (f32[8,16,8,128]{3,2,1,0:T(8,128)S(1)}, f32[8,16,8,128]{3,2,1,0:T(8,128)}, u32[]{:S(2)}) copy-start(f32[8,16,8,128]{3,2,1,0:T(8,128)} %a.1) | copy-start | bytes 1572868
  1.0 0.8 %copy-start.1 = (f32[8,16,128]{2,1,0:T(8,128)S(1)}, f32[8,16,128]{2,1,0:T(8,128)}, u32[]{:S(2)}) copy-start(f32[8,16,128]{2,1,0:T(8,128)} %innov.1) | copy-start | bytes 196612
  1.9 0.8 %copy-start.2 = (f32[16,8,128]{2,1,0:T(8,128)S(1)}, f32[16,8,128]{2,1,0:T(8,128)}, u32[]{:S(2)}) copy-start(f32[16,8,128]{2,1,0:T(8,128)} %dif.1) | copy-start | bytes 196612
  2.7 0.8 %copy-start.3 = (f32[16,8,128]{2,1,0:T(8,128)S(1)}, f32[16,8,128]{2,1,0:T(8,128)}, u32[]{:S(2)}) copy-start(f32[16,8,128]{2,1,0:T(8,128)} %wx.1) | copy-start | bytes 196612
  3.6 0.8 %copy-start.4 = (f32[16,8,128]{2,1,0:T(8,128)S(1)}, f32[16,8,128]{2,1,0:T(8,128)}, u32[]{:S(2)}) copy-start(f32[16,8,128]{2,1,0:T(8,128)} %wy.1) | copy-start | bytes 196612
  4.4 0.8 %copy-start.5 = (f32[16,8,128]{2,1,0:T(8,128)S(1)}, f32[16,8,128]{2,1,0:T(8,128)}, u32[]{:S(2)}) copy-start(f32[16,8,128]{2,1,0:T(8,128)} %vm.1) | copy-start | bytes 196612
  5.2 0.7 %copy-start.6 = (s32[8,128]{1,0:T(8,128)S(1)}, s32[8,128]{1,0:T(8,128)}, u32[]{:S(2)}) copy-start(s32[8,128]{1,0:T(8,128)} %cells.1) | copy-start | bytes 12292

commit v2 on v1

v2 whole, which is shorter than its diff:
```python
import functools

import jax
import jax.numpy as jnp
from jax import lax
from jax.experimental import pallas as pl
from jax.experimental.pallas import tpu as pltpu
from jax.sharding import PartitionSpec as P

MESH = pl.DeviceIdType.MESH

LEV = 16
TX = 8
NY = 128
STEPS_DEV = 8
DEPTH = 5
CIRC_ALPHA = 0.1

RATES, FORWARD, INNOV, CELLS, STATE, INNOV_UP, CELLS_UP, RELAY, PER_SIDE = 0, 4, 8, 9, 10, 18, 19, 20, 25
INNOV_T, CELLS_T, STATE_T = 2 * PER_SIDE, 2 * PER_SIDE + 1, 2 * PER_SIDE + 2
TRANSFERS = STATE_T + DEPTH
OWN = STEPS_DEV - DEPTH


def fill_forcing(forcing, which, plane, parts):
    x_of = lax.broadcasted_iota(jnp.int32, (TX, NY), 0)
    y_of = lax.broadcasted_iota(jnp.int32, (NY, NY), 0)
    total = None
    for values, cells, low, high in parts:
        column = cells // NY
        row = cells % NY
        mask = (column == x_of) & (x_of >= low) & (x_of < high)
        head = values.astype(jnp.bfloat16).astype(jnp.float32)
        rest = values - head
        pieces = [
            jnp.where(mask[None], piece[:, None, :], 0.0).reshape(LEV * TX, NY).astype(jnp.bfloat16)
            for piece in (head, rest)
        ]
        hot = jnp.where(row == y_of, 1.0, 0.0).astype(jnp.bfloat16)
        part = lax.dot_general(
            jnp.concatenate(pieces, axis=1),
            jnp.concatenate([hot, hot], axis=1),
            (((1,), (1,)), ((), ())),
            preferred_element_type=jnp.float32,
        )
        total = part if total is None else total + part
    forcing[plane, :, which] = total.reshape(LEV, TX, NY)


def kernel(
    time_parts, tiles,
    a, innov, cells, dif, wx, wy, vm, out,
    ac, hl, hr, nc, nl, nr, kc, kl, kr, kc2, kl2, kr2, rc, rl, rr, coef, forcing, va, vb, ob,
    send, recv, local,
):
    t = lax.axis_index("tm")
    s = lax.axis_index("space")
    before = lax.rem(t + time_parts - 1, time_parts)
    after = lax.rem(t + 1, time_parts)
    core = lax.rem(t, 2)
    sibling = t + 1 - 2 * core
    mid = tiles // 2
    has_left = s > 0
    has_right = s < tiles - 1
    is_last = t == time_parts - 1

    barrier = pltpu.get_barrier_semaphore()

    def greet(device):
        pl.semaphore_signal(barrier, inc=1, device_id=device, device_id_type=MESH)

    greet((after, s))
    greet((sibling, s))
    for here, device in (
        (has_left, s - 1),
        (has_right, s + 1),
        (s == 0, mid - 1),
        (s == tiles - 1, mid),
        (s == mid, 0),
        (s == mid - 1, tiles - 1),
    ):

        @pl.when(here)
        def _(device=device):
            greet((t, device))

    fields = (dif, wx, wy, vm)
    loads = [
        pltpu.make_async_copy(innov, nc.at[pl.ds(0, STEPS_DEV)], local.at[0]),
        pltpu.make_async_copy(cells, kc, local.at[1]),
        pltpu.make_async_copy(a.at[pl.ds(DEPTH, OWN)], ac.at[pl.ds(0, OWN)], local.at[2]),
    ] + [pltpu.make_async_copy(f, rc.at[i], local.at[3 + i]) for i, f in enumerate(fields)]
    for load in loads:
        load.start()

    def remote(number, src, dst, device, landing=None):
        return pltpu.make_async_remote_copy(
            src_ref=src, dst_ref=dst, send_sem=send.at[number],
            recv_sem=recv.at[number if landing is None else landing],
            device_id=device, device_id_type=MESH,
        )

    class Side:
        def __init__(self, base, step, first, halo, inn, cel, cel_up, rat, relay, entry):
            self.sends, self.receives = (has_right, has_left) if step > 0 else (has_left, has_right)
            self.zeros = (halo.at[pl.ds(0, OWN)], inn, cel, cel_up, rat)
            to = (t, s + step)
            cols = pl.ds(first, 5)
            edge = pl.ds(4, 4) if step > 0 else pl.ds(0, 4)
            cut = [cols if i < 2 else edge for i in range(4)]
            self.rates = [
                remote(base + RATES + i, f.at[:, cut[i]], rat.at[i, :, cut[i]], to)
                for i, f in enumerate(fields)
            ]
            self.forward = [
                remote(base + FORWARD + i, rat.at[i, :, cut[i]], rat.at[i, :, cut[i]], (sibling, s), base + RATES + i)
                for i in range(4)
            ]
            self.early = [
                remote(base + CELLS, cells, cel, to),
                remote(base + INNOV, innov, inn.at[pl.ds(0, STEPS_DEV)], to),
            ]
            self.late = [
                remote(base + CELLS_UP, kc2, cel_up, to),
                remote(base + INNOV_UP, nc.at[pl.ds(STEPS_DEV, 4)], inn.at[pl.ds(STEPS_DEV, 4)], to),
            ]
            self.is_relay = s == relay
            late_to = (t, jnp.where(s == entry, relay, s + step))
            self.state = [
                remote(base + STATE + i, a.at[i + DEPTH, :, cols], halo.at[i, :, cols], to)
                for i in range(OWN)
            ] + [
                remote(base + STATE + i, ac.at[i, :, cols], halo.at[i, :, cols], late_to)
                for i in range(OWN, STEPS_DEV)
            ]
            self.relayed = [
                remote(base + RELAY + i - OWN, halo.at[i, :, cols], halo.at[i, :, cols], (t, entry + step), base + STATE + i)
                for i in range(OWN, STEPS_DEV)
            ]

    sides = (
        Side(0, 1, 3, hl, nl, kl, kl2, rl, 0, mid - 1),
        Side(PER_SIDE, -1, 0, hr, nr, kr, kr2, rr, tiles - 1, mid),
    )
    up_early = [
        remote(CELLS_T, cells, kc2, (before, s)),
        remote(INNOV_T, innov.at[pl.ds(0, 4)], nc.at[pl.ds(STEPS_DEV, 4)], (before, s)),
    ]
    up_state = [remote(STATE_T + i, a.at[i], ac.at[OWN + i], (before, s)) for i in range(DEPTH)]

    for side in sides:

        @pl.when(jnp.logical_not(side.receives))
        def _(side=side):
            for ref in side.zeros:
                ref[...] = jnp.zeros(ref.shape, ref.dtype)

    def each(condition, copies, act):
        @pl.when(condition)
        def _():
            for copy in copies:
                act(copy)

    def begin(copy):
        copy.start()

    def arrive(copy):
        copy.wait_recv()

    def leave(copy):
        copy.wait_send()

    def number(flag):
        return flag.astype(jnp.int32)

    pl.semaphore_wait(
        barrier,
        2 + number(has_left) + number(has_right) + number(s == 0) + number(s == tiles - 1)
        + number(s == mid) + number(s == mid - 1),
    )
    for copy in up_early + up_state:
        copy.start()
    for side in sides:
        each(side.sends, side.early, begin)
    for side in sides:
        for half in range(2):
            each(side.sends & (core == half), side.rates[2 * half : 2 * half + 2], begin)
    for i in range(OWN):
        for side in sides:
            each(side.sends, [side.state[i]], begin)

    for load in loads:
        load.wait()

    def own_forcing(n, carry):
        fill_forcing(forcing, 0, n, [(nc[n], kc[pl.ds(n, 1)], 0, TX)])
        return carry

    lax.fori_loop(0, STEPS_DEV, own_forcing, 0)

    def pass_on():
        for copy in up_early:
            copy.wait_recv()
        for side in sides:
            each(side.sends, side.late, begin)
        for i in range(DEPTH):
            up_state[i].wait_recv()
            for side in sides:
                each(side.sends, [side.state[OWN + i]], begin)

    pl.when(core == 0)(pass_on)

    for side in sides:
        for half in range(2):
            mine = slice(2 * half, 2 * half + 2)
            each(side.receives & (core == half), side.rates[mine], arrive)
            each(side.receives & (core == half), side.forward[mine], begin)
    for side in sides:
        for half in range(2):
            other = slice(2 - 2 * half, 4 - 2 * half)
            each(side.receives & (core == half), side.rates[other], arrive)

    x_of = lax.broadcasted_iota(jnp.int32, (TX, NY), 0)
    y_of = lax.broadcasted_iota(jnp.int32, (TX, NY), 1)
    first_half = x_of < 4
    is_first, is_end = x_of == 0, x_of == TX - 1

    def down_x(v):
        return pltpu.roll(v, 1, 0)

    def up_x(v):
        return pltpu.roll(v, TX - 1, 0)

    def make_rates(l, carry):
        def own(part):
            return part[0, l], part[1, l], part[2, l], part[3, l]

        dc, xc, yc, mc = own(rc)
        dl, xl, yl, ml = own(rl)
        dr, xr, yr, mr = own(rr)
        east_c, west_c = dc + jnp.maximum(-xc, 0.0), dc + jnp.maximum(xc, 0.0)
        east_l, west_l = dl + jnp.maximum(-xl, 0.0), dl + jnp.maximum(xl, 0.0)
        east_r, west_r = dr + jnp.maximum(-xr, 0.0), dr + jnp.maximum(xr, 0.0)
        dh = jnp.where(first_half, dr, dl)
        yh = jnp.where(first_half, yr, yl)
        mh = jnp.where(first_half, mr, ml)
        east_h = jnp.where(first_half, east_r, east_l)
        west_h = jnp.where(first_half, west_r, west_l)
        from_west = (
            jnp.where(is_first, down_x(east_l), down_x(east_c)),
            jnp.where(first_half, jnp.where(is_first, down_x(east_c), down_x(east_r)), down_x(east_l)),
        )
        from_east = (
            jnp.where(is_end, up_x(west_r), up_x(west_c)),
            jnp.where(first_half, up_x(west_r), jnp.where(is_end, up_x(west_c), up_x(west_l))),
        )
        for which, (d, e, w, y, m) in enumerate(
            ((dc, east_c, west_c, yc, mc), (dh, east_h, west_h, yh, mh))
        ):
            north, south = d + jnp.maximum(-y, 0.0), d + jnp.maximum(y, 0.0)
            coef[l, which, 0] = 1.0 - (e + w + north + south + m + m)
            coef[l, which, 1] = from_west[which]
            coef[l, which, 2] = from_east[which]
            coef[l, which, 3] = jnp.where(y_of == 0, 0.0, pltpu.roll(north, 1, 1))
            coef[l, which, 4] = jnp.where(y_of == NY - 1, 0.0, pltpu.roll(south, NY - 1, 1))
            coef[l, which, 5] = m
        return carry

    lax.fori_loop(0, LEV, make_rates, 0)

    for side in sides:
        each(side.receives, side.early, arrive)

    def halo_forcing(n, carry):
        fill_forcing(forcing, 1, n, [(nl[n], kl[pl.ds(n, 1)], 4, TX), (nr[n], kr[pl.ds(n, 1)], 0, 4)])
        return carry

    lax.fori_loop(1, STEPS_DEV, halo_forcing, 0)
    pl.when(core == 1)(pass_on)

    def next_forcing(n):
        m = n + STEPS_DEV
        fill_forcing(forcing, 0, m, [(nc[m], kc2[pl.ds(n, 1)], 0, TX)])
        fill_forcing(forcing, 1, m, [(nl[m], kl2[pl.ds(n, 1)], 4, TX), (nr[m], kr2[pl.ds(n, 1)], 0, 4)])

    def sweep(i, load, dst, plane, last):
        def level(l):
            c, h = load(l)
            whole = h
            if isinstance(h, tuple):
                whole = jnp.where(first_half, h[1], h[0])
            tiles = [(c, whole), (coef[l, 0, 5] * c, None if last else coef[l, 1, 5] * whole)]
            return c, h, whole, tiles[1]

        levels = [level(0), level(1)]
        for l in range(LEV):
            if 0 < l < LEV - 1:
                levels.append(level(l + 1))
            c, h, whole, _ = levels[l]
            cd, cu = down_x(c), up_x(c)
            if isinstance(h, tuple):
                ld, rd, lu, ru = down_x(h[0]), down_x(h[1]), up_x(h[0]), up_x(h[1])
                hd, hu = jnp.where(first_half, rd, ld), jnp.where(first_half, ru, lu)
            else:
                hd, hu = down_x(whole), up_x(whole)
                ld, ru = hd, hu
            todo = [(0, c, jnp.where(is_first, ld, cd), jnp.where(is_end, ru, cu))]
            if not last:
                todo.append((1, whole, jnp.where(is_first, cd, hd), jnp.where(is_end, cu, hu)))
            for which, v, west, east in todo:
                total = forcing[plane, l, which] + coef[l, which, 0] * v
                total = total + (coef[l, which, 1] * west + coef[l, which, 2] * east)
                total = total + (
                    coef[l, which, 3] * pltpu.roll(v, 1, 1) + coef[l, which, 4] * pltpu.roll(v, NY - 1, 1)
                )
                for k in (l - 1, l + 1):
                    if 0 <= k < LEV:
                        total = total + levels[k][3][which]
                if last:
                    ob[i, l] = total
                else:
                    dst[l, which] = total

    def chain(i, carry):
        for k in range(STEPS_DEV):
            for side in sides:
                each(side.receives & (i == k), [side.state[k]], arrive)

        @pl.when(i == OWN)
        def _():
            for k in range(DEPTH):
                for side in sides:
                    each(side.is_relay, [side.state[OWN + k]], arrive)
                    each(side.is_relay, [side.relayed[k]], begin)

        @pl.when(i == OWN + 1)
        def _():
            for side in sides:
                each(side.receives, side.late, arrive)

        @pl.when(i > OWN)
        def _():
            next_forcing(i - OWN - 1)

        sweep(i, lambda l: (ac[i, l], (hl[i, l], hr[i, l])), va, i + 4, False)

        @pl.when(is_last & (i == OWN))
        def _():
            va[...] = forcing[STEPS_DEV - 1]

        bufs = (va, vb)
        for k in range(2, DEPTH + 1):
            src, dst = bufs[k % 2], bufs[(k + 1) % 2]

            @pl.when(is_last & (i == k + 2))
            def _(src=src):
                src[:, 0] = CIRC_ALPHA * (src[:, 0] - ac[OWN])
                outside = jnp.where(first_half[None], hr[OWN], hl[OWN])
                src[:, 1] = CIRC_ALPHA * (src[:, 1] - outside)

            sweep(i, lambda l, src=src: (src[l, 0], src[l, 1]), dst, i + DEPTH - k, k == DEPTH)
        pltpu.make_async_copy(ob.at[i], out.at[i], local.at[7 + i]).start()
        return carry

    lax.fori_loop(0, STEPS_DEV, chain, 0)

    for i in range(STEPS_DEV):
        pltpu.make_async_copy(ob.at[i], out.at[i], local.at[7 + i]).wait()
    for side in sides:
        each(side.sends, side.early + side.late + side.state, leave)
        each(side.is_relay, side.relayed, leave)
        for half in range(2):
            mine = slice(2 * half, 2 * half + 2)
            each(side.sends & (core == half), side.rates[mine], leave)
            each(side.receives & (core == half), side.forward[mine], leave)
    for copy in up_early + up_state:
        copy.wait_send()


def body(adjoint_iterate, innovations, station_cells, diffusivity, wind_x, wind_y, vertical_mixing):
    field = (LEV, TX, NY)
    f32, i32 = jnp.float32, jnp.int32
    scratch = (
        [pltpu.VMEM((STEPS_DEV,) + field, f32)] * 3
        + [pltpu.VMEM((STEPS_DEV + 4, LEV, NY), f32)] * 3
        + [pltpu.VMEM((STEPS_DEV, NY), i32)] * 6
        + [pltpu.VMEM((4,) + field, f32)] * 3
        + [pltpu.VMEM((LEV, 2, 6, TX, NY), f32)]
        + [pltpu.VMEM((STEPS_DEV + 4, LEV, 2, TX, NY), f32)]
        + [pltpu.VMEM((LEV, 2, TX, NY), f32)] * 2
        + [pltpu.VMEM((STEPS_DEV,) + field, f32)]
        + [pltpu.SemaphoreType.DMA((TRANSFERS,))] * 2
        + [pltpu.SemaphoreType.DMA((7 + STEPS_DEV,))]
    )
    return pl.pallas_call(
        functools.partial(kernel, lax.axis_size("tm"), lax.axis_size("space")),
        out_shape=jax.ShapeDtypeStruct((STEPS_DEV,) + field, f32),
        in_specs=[pl.BlockSpec(memory_space=pl.ANY)] * 7,
        out_specs=pl.BlockSpec(memory_space=pl.ANY),
        scratch_shapes=scratch,
        compiler_params=pltpu.CompilerParams(
            collective_id=0, has_side_effects=True, vmem_limit_bytes=62 * 2**20
        ),
        name="update",
    )(adjoint_iterate, innovations, station_cells, diffusivity, wind_x, wind_y, vertical_mixing)


def solution(mesh):
    in_specs = (
        P("tm", None, "space", None),
        P("tm", None, "space"),
        P("tm", "space"),
        P(None, "space", None),
        P(None, "space", None),
        P(None, "space", None),
        P(None, "space", None),
    )
    out_specs = P("tm", None, "space", None)
    return jax.shard_map(body, mesh=mesh, in_specs=in_specs, out_specs=out_specs, check_vma=False)
```

time: 38.4 us -> 32 us (0.83)
  the two profiles are of different devices: /device:TPU:29 before, /device:TPU:1 now
where the time goes in v2:
time: 32 us; the launch traced here: 31.9 us
  Pallas kernels  30 us (94%)
  local copies, waits for them, and re-layouts  1.87 us (6%)
    pallas_call x1, Pallas kernels, body(): pl.pallas_call(functools.partial(kernel, lax.axis_size('tm'), lax.axis_si...  30 us
    unnamed x1, local copies, waits for them, and re-layouts  1.87 us

profile of v2, /device:TPU:1, one launch (start us, length us, event | category | flops | bytes accessed | tf_op | source)
XLA Modules:
  0.0 31.9 jit_solution(16447551981865327175)
XLA Ops:
  0.0 30.0 %update.1 = f32[8,16,8,128]{3,2,1,0:T(8,128)} custom-call(f32[8,16,8,128]{3,2,1,0:T(8,128)} %a.1, f32[8,16,128]{2,1,0:T(8,128)} %innov.1, s32[8,128]{1,0:T(8,128)} %cells.1, f32[16,8,128]{2,1,0:T(8,128)} %dif.1, f32[16,8,128]{2,1,0:T(8,128)} %wx.1, f32[16,8,128]{2,1,0:T(8,128)} %wy.1, f32[16,8,128]{2,1,0:T(8,128)} %vm.1), custom_call_target="tpu_custom_call" | custom-call | tf_op jit(solution)/shard_map/update/pallas_call | solution.py:395
  30.0 1.9 %copy.9 = f32[8,16,8,128]{3,2,1,0:T(8,128)} copy(f32[8,16,8,128]{3,2,1,0:T(8,128)} %update.1) | data formatting | bytes 1048576

commit v3 on v2

--- a/solution.py
+++ b/solution.py
@@ -15,8 +15,9 @@
 STEPS_DEV = 8
 DEPTH = 5
 CIRC_ALPHA = 0.1
-
-RATES, FORWARD, INNOV, CELLS, STATE, INNOV_UP, CELLS_UP, RELAY, PER_SIDE = 0, 4, 8, 9, 10, 18, 19, 20, 25
+GROUP = 2
+
+RATES, FORWARD, INNOV, CELLS, STATE, INNOV_UP, CELLS_UP, RELAY, PER_SIDE = 0, 4, 8, 9, 10, 18, 19, 20, 23
 INNOV_T, CELLS_T, STATE_T = 2 * PER_SIDE, 2 * PER_SIDE + 1, 2 * PER_SIDE + 2
 TRANSFERS = STATE_T + DEPTH
 OWN = STEPS_DEV - DEPTH
@@ -50,8 +51,8 @@
 def kernel(
     time_parts, tiles,
     a, innov, cells, dif, wx, wy, vm, out,
-    ac, hl, hr, nc, nl, nr, kc, kl, kr, kc2, kl2, kr2, rc, rl, rr, coef, forcing, va, vb, ob,
-    send, recv, local,
+    ac, hl, hr, nc, nl, nr, kc, kl, kr, kc2, kl2, kr2, rc, rl, rr, coef, forcing, va, vb, ob, hold,
+    send, recv, local, ready,
 ):
     t = lax.axis_index("tm")
     s = lax.axis_index("space")
@@ -75,9 +76,9 @@
         (has_left, s - 1),
         (has_right, s + 1),
         (s == 0, mid - 1),
-        (s == tiles - 1, mid),
-        (s == mid, 0),
-        (s == mid - 1, tiles - 1),
+        (s == 0, mid),
+        (s == tiles - 1, mid - 1),
+        (s == mid, tiles - 1),
     ):
 
         @pl.when(here)
@@ -103,7 +104,7 @@
     class Side:
         def __init__(self, base, step, first, halo, inn, cel, cel_up, rat, relay, entry):
             self.sends, self.receives = (has_right, has_left) if step > 0 else (has_left, has_right)
-            self.zeros = (halo.at[pl.ds(0, OWN)], inn, cel, cel_up, rat)
+            self.zeros = (halo, inn, cel, cel_up, rat)
             to = (t, s + step)
             cols = pl.ds(first, 5)
             edge = pl.ds(4, 4) if step > 0 else pl.ds(0, 4)
@@ -124,23 +125,26 @@
                 remote(base + CELLS_UP, kc2, cel_up, to),
                 remote(base + INNOV_UP, nc.at[pl.ds(STEPS_DEV, 4)], inn.at[pl.ds(STEPS_DEV, 4)], to),
             ]
-            self.is_relay = s == relay
-            late_to = (t, jnp.where(s == entry, relay, s + step))
+            self.is_relay, self.is_entry = s == relay, s == entry
             self.state = [
                 remote(base + STATE + i, a.at[i + DEPTH, :, cols], halo.at[i, :, cols], to)
                 for i in range(OWN)
             ] + [
-                remote(base + STATE + i, ac.at[i, :, cols], halo.at[i, :, cols], late_to)
+                remote(base + STATE + i, ac.at[i, :, cols], halo.at[i, :, cols], to)
                 for i in range(OWN, STEPS_DEV)
             ]
+            self.detour = [
+                remote(base + STATE + i, a.at[i + DEPTH, :, cols], hold.at[i, :, cols], (t, relay), base + RELAY + i)
+                for i in range(OWN)
+            ]
             self.relayed = [
-                remote(base + RELAY + i - OWN, halo.at[i, :, cols], halo.at[i, :, cols], (t, entry + step), base + STATE + i)
-                for i in range(OWN, STEPS_DEV)
+                remote(base + RELAY + i, hold.at[i, :, cols], halo.at[i, :, cols], (t, entry + step), base + STATE + i)
+                for i in range(OWN)
             ]
 
     sides = (
-        Side(0, 1, 3, hl, nl, kl, kl2, rl, 0, mid - 1),
-        Side(PER_SIDE, -1, 0, hr, nr, kr, kr2, rr, tiles - 1, mid),
+        Side(0, 1, 3, hl, nl, kl, kl2, rl, tiles - 1, mid - 1),
+        Side(PER_SIDE, -1, 0, hr, nr, kr, kr2, rr, 0, mid),
     )
     up_early = [
         remote(CELLS_T, cells, kc2, (before, s)),
@@ -175,40 +179,49 @@
 
     pl.semaphore_wait(
         barrier,
-        2 + number(has_left) + number(has_right) + number(s == 0) + number(s == tiles - 1)
-        + number(s == mid) + number(s == mid - 1),
+        2 + number(has_left) + number(has_right) + 2 * number(s == mid - 1) + number(s == mid)
+        + number(s == tiles - 1),
     )
+
+    @pl.when(s == mid - 1)
+    def _():
+        pl.semaphore_signal(ready, inc=1, device_id=(t, 0), device_id_type=MESH)
+
     for copy in up_early + up_state:
         copy.start()
     for side in sides:
         each(side.sends, side.early, begin)
+        each(side.is_entry, side.detour, begin)
     for side in sides:
         for half in range(2):
             each(side.sends & (core == half), side.rates[2 * half : 2 * half + 2], begin)
+
+    for load in loads:
+        load.wait()
     for i in range(OWN):
         for side in sides:
-            each(side.sends, [side.state[i]], begin)
-
-    for load in loads:
-        load.wait()
+            each(side.sends & jnp.logical_not(side.is_entry), [side.state[i]], begin)
 
     def own_forcing(n, carry):
         fill_forcing(forcing, 0, n, [(nc[n], kc[pl.ds(n, 1)], 0, TX)])
         return carry
 
-    lax.fori_loop(0, STEPS_DEV, own_forcing, 0)
-
-    def pass_on():
-        for copy in up_early:
-            copy.wait_recv()
-        for side in sides:
-            each(side.sends, side.late, begin)
-        for i in range(DEPTH):
+    lax.fori_loop(0, STEPS_DEV, own_forcing, 0, unroll=4)
+
+    def pass_on(first, last):
+        if first == 0:
+            for copy in up_early:
+                copy.wait_recv()
+            for side in sides:
+                each(side.sends, side.late, begin)
+        for i in range(first, last):
             up_state[i].wait_recv()
             for side in sides:
                 each(side.sends, [side.state[OWN + i]], begin)
 
-    pl.when(core == 0)(pass_on)
+    @pl.when(core == 0)
+    def _():
+        pass_on(0, DEPTH)
 
     for side in sides:
         for half in range(2):
@@ -266,7 +279,18 @@
             coef[l, which, 5] = m
         return carry
 
-    lax.fori_loop(0, LEV, make_rates, 0)
+    lax.fori_loop(0, LEV, make_rates, 0, unroll=2)
+
+    def relay(side):
+        for i in range(OWN):
+            each(side.is_relay, [side.detour[i]], arrive)
+            each(side.is_relay, [side.relayed[i]], begin)
+
+    relay(sides[0])
+
+    @pl.when(core == 1)
+    def _():
+        pass_on(0, 2)
 
     for side in sides:
         each(side.receives, side.early, arrive)
@@ -275,99 +299,121 @@
         fill_forcing(forcing, 1, n, [(nl[n], kl[pl.ds(n, 1)], 4, TX), (nr[n], kr[pl.ds(n, 1)], 0, 4)])
         return carry
 
-    lax.fori_loop(1, STEPS_DEV, halo_forcing, 0)
-    pl.when(core == 1)(pass_on)
+    lax.fori_loop(0, STEPS_DEV, halo_forcing, 0, unroll=4)
+
+    @pl.when(core == 1)
+    def _():
+        pass_on(2, DEPTH)
+
+    @pl.when(s == 0)
+    def _():
+        pl.semaphore_wait(ready, 1)
+
+    relay(sides[1])
+
 
     def next_forcing(n):
         m = n + STEPS_DEV
         fill_forcing(forcing, 0, m, [(nc[m], kc2[pl.ds(n, 1)], 0, TX)])
         fill_forcing(forcing, 1, m, [(nl[m], kl2[pl.ds(n, 1)], 4, TX), (nr[m], kr2[pl.ds(n, 1)], 0, 4)])
 
-    def sweep(i, load, dst, plane, last):
+    def sweep(first, loads, dst, plane, last):
         def level(l):
-            c, h = load(l)
-            whole = h
-            if isinstance(h, tuple):
-                whole = jnp.where(first_half, h[1], h[0])
-            tiles = [(c, whole), (coef[l, 0, 5] * c, None if last else coef[l, 1, 5] * whole)]
-            return c, h, whole, tiles[1]
+            own_mix = coef[l, 0, 5]
+            halo_mix = None if last else coef[l, 1, 5]
+            found = []
+            for load in loads:
+                c, h = load(l)
+                whole = h
+                if isinstance(h, tuple):
+                    whole = jnp.where(first_half, h[1], h[0])
+                found.append((c, h, whole, (own_mix * c, None if last else halo_mix * whole)))
+            return found
 
         levels = [level(0), level(1)]
         for l in range(LEV):
             if 0 < l < LEV - 1:
                 levels.append(level(l + 1))
-            c, h, whole, _ = levels[l]
-            cd, cu = down_x(c), up_x(c)
-            if isinstance(h, tuple):
-                ld, rd, lu, ru = down_x(h[0]), down_x(h[1]), up_x(h[0]), up_x(h[1])
-                hd, hu = jnp.where(first_half, rd, ld), jnp.where(first_half, ru, lu)
-            else:
-                hd, hu = down_x(whole), up_x(whole)
-                ld, ru = hd, hu
-            todo = [(0, c, jnp.where(is_first, ld, cd), jnp.where(is_end, ru, cu))]
-            if not last:
-                todo.append((1, whole, jnp.where(is_first, cd, hd), jnp.where(is_end, cu, hu)))
-            for which, v, west, east in todo:
-                total = forcing[plane, l, which] + coef[l, which, 0] * v
-                total = total + (coef[l, which, 1] * west + coef[l, which, 2] * east)
-                total = total + (
-                    coef[l, which, 3] * pltpu.roll(v, 1, 1) + coef[l, which, 4] * pltpu.roll(v, NY - 1, 1)
-                )
-                for k in (l - 1, l + 1):
-                    if 0 <= k < LEV:
-                        total = total + levels[k][3][which]
-                if last:
-                    ob[i, l] = total
+            factor = [[coef[l, which, k] for k in range(5)] for which in range(1 if last else 2)]
+            for p in range(GROUP):
+                c, h, whole, _ = levels[l][p]
+                cd, cu = down_x(c), up_x(c)
+                if isinstance(h, tuple):
+                    ld, rd, lu, ru = down_x(h[0]), down_x(h[1]), up_x(h[0]), up_x(h[1])
+                    hd, hu = jnp.where(first_half, rd, ld), jnp.where(first_half, ru, lu)
                 else:
-                    dst[l, which] = total
-
-    def chain(i, carry):
+                    hd, hu = down_x(whole), up_x(whole)
+                    ld, ru = hd, hu
+                todo = [(c, jnp.where(is_first, ld, cd), jnp.where(is_end, ru, cu))]
+                if not last:
+                    todo.append((whole, jnp.where(is_first, cd, hd), jnp.where(is_end, cu, hu)))
+                for which, (v, west, east) in enumerate(todo):
+                    keep, from_west, from_east, from_south, from_north = factor[which]
+                    total = forcing[plane + p, l, which] + keep * v
+                    total = total + (from_west * west + from_east * east)
+                    total = total + (
+                        from_south * pltpu.roll(v, 1, 1) + from_north * pltpu.roll(v, NY - 1, 1)
+                    )
+                    for k in (l - 1, l + 1):
+                        if 0 <= k < LEV:
+                            total = total + levels[k][p][3][which]
+                    if last:
+                        ob[first + p, l] = total
+                    else:
+                        dst[p, l, which] = total
+
+    def chain(group, carry):
+        first = group * GROUP
         for k in range(STEPS_DEV):
             for side in sides:
-                each(side.receives & (i == k), [side.state[k]], arrive)
-
-        @pl.when(i == OWN)
-        def _():
-            for k in range(DEPTH):
-                for side in sides:
-                    each(side.is_relay, [side.state[OWN + k]], arrive)
-                    each(side.is_relay, [side.relayed[k]], begin)
-
-        @pl.when(i == OWN + 1)
+                each(side.receives & (group == k // GROUP), [side.state[k]], arrive)
+
+        @pl.when(group == (OWN + 1) // GROUP)
         def _():
             for side in sides:
                 each(side.receives, side.late, arrive)
 
-        @pl.when(i > OWN)
+        for p in range(GROUP):
+
+            @pl.when(first + p > OWN)
+            def _(p=p):
+                next_forcing(first + p - OWN - 1)
+
+        def start(p):
+            return lambda l: (ac[first + p, l], (hl[first + p, l], hr[first + p, l]))
+
+        sweep(first, [start(p) for p in range(GROUP)], va, first + 4, False)
+
+        @pl.when(is_last & (group == OWN // GROUP))
         def _():
-            next_forcing(i - OWN - 1)
-
-        sweep(i, lambda l: (ac[i, l], (hl[i, l], hr[i, l])), va, i + 4, False)
-
-        @pl.when(is_last & (i == OWN))
-        def _():
-            va[...] = forcing[STEPS_DEV - 1]
+            va[OWN % GROUP] = forcing[STEPS_DEV - 1]
 
         bufs = (va, vb)
         for k in range(2, DEPTH + 1):
             src, dst = bufs[k % 2], bufs[(k + 1) % 2]
 
-            @pl.when(is_last & (i == k + 2))
-            def _(src=src):
-                src[:, 0] = CIRC_ALPHA * (src[:, 0] - ac[OWN])
+            @pl.when(is_last & (group == (k + 2) // GROUP))
+            def _(src=src, p=(k + 2) % GROUP):
+                src[p, :, 0] = CIRC_ALPHA * (src[p, :, 0] - ac[OWN])
                 outside = jnp.where(first_half[None], hr[OWN], hl[OWN])
-                src[:, 1] = CIRC_ALPHA * (src[:, 1] - outside)
-
-            sweep(i, lambda l, src=src: (src[l, 0], src[l, 1]), dst, i + DEPTH - k, k == DEPTH)
-        pltpu.make_async_copy(ob.at[i], out.at[i], local.at[7 + i]).start()
+                src[p, :, 1] = CIRC_ALPHA * (src[p, :, 1] - outside)
+
+            def middle(p, src=src):
+                return lambda l: (src[p, l, 0], src[p, l, 1])
+
+            sweep(first, [middle(p) for p in range(GROUP)], dst, first + DEPTH - k, k == DEPTH)
+        for p in range(GROUP):
+            pltpu.make_async_copy(ob.at[first + p], out.at[first + p], local.at[7 + first + p]).start()
         return carry
 
-    lax.fori_loop(0, STEPS_DEV, chain, 0)
+    lax.fori_loop(0, STEPS_DEV // GROUP, chain, 0)
 
     for i in range(STEPS_DEV):
         pltpu.make_async_copy(ob.at[i], out.at[i], local.at[7 + i]).wait()
     for side in sides:
-        each(side.sends, side.early + side.late + side.state, leave)
+        each(side.sends, side.early + side.late + side.state[OWN:], leave)
+        each(side.sends & jnp.logical_not(side.is_entry), side.state[:OWN], leave)
+        each(side.is_entry, side.detour, leave)
         each(side.is_relay, side.relayed, leave)
         for half in range(2):
             mine = slice(2 * half, 2 * half + 2)
@@ -387,10 +433,10 @@
         + [pltpu.VMEM((4,) + field, f32)] * 3
         + [pltpu.VMEM((LEV, 2, 6, TX, NY), f32)]
         + [pltpu.VMEM((STEPS_DEV + 4, LEV, 2, TX, NY), f32)]
-        + [pltpu.VMEM((LEV, 2, TX, NY), f32)] * 2
-        + [pltpu.VMEM((STEPS_DEV,) + field, f32)]
+        + [pltpu.VMEM((GROUP, LEV, 2, TX, NY), f32)] * 2
+        + [pltpu.VMEM((STEPS_DEV,) + field, f32), pltpu.VMEM((OWN,) + field, f32)]
         + [pltpu.SemaphoreType.DMA((TRANSFERS,))] * 2
-        + [pltpu.SemaphoreType.DMA((7 + STEPS_DEV,))]
+        + [pltpu.SemaphoreType.DMA((7 + STEPS_DEV,)), pltpu.SemaphoreType.REGULAR]
     )
     return pl.pallas_call(
         functools.partial(kernel, lax.axis_size("tm"), lax.axis_size("space")),

time: 32 us -> 28.7 us (0.90)
  the two profiles are of different devices: /device:TPU:1 before, /device:TPU:2 now
where the time goes in v3:
time: 28.7 us; the launch traced here: 28.6 us
  Pallas kernels  26.7 us (93%)
  local copies, waits for them, and re-layouts  1.87 us (7%)
    pallas_call x1, Pallas kernels, body(): pl.pallas_call(functools.partial(kernel, lax.axis_size('tm'), lax.axis_si...  26.7 us
    unnamed x1, local copies, waits for them, and re-layouts  1.87 us

profile of v3, /device:TPU:2, one launch (start us, length us, event | category | flops | bytes accessed | tf_op | source)
XLA Modules:
  0.0 28.6 jit_solution(9509355252560900271)
XLA Ops:
  0.0 26.7 %update.1 = f32[8,16,8,128]{3,2,1,0:T(8,128)} custom-call(f32[8,16,8,128]{3,2,1,0:T(8,128)} %a.1, f32[8,16,128]{2,1,0:T(8,128)} %innov.1, s32[8,128]{1,0:T(8,128)} %cells.1, f32[16,8,128]{2,1,0:T(8,128)} %dif.1, f32[16,8,128]{2,1,0:T(8,128)} %wx.1, f32[16,8,128]{2,1,0:T(8,128)} %wy.1, f32[16,8,128]{2,1,0:T(8,128)} %vm.1), custom_call_target="tpu_custom_call" | custom-call | tf_op jit(solution)/shard_map/update/pallas_call | solution.py:441
  26.7 1.9 %copy.9 = f32[8,16,8,128]{3,2,1,0:T(8,128)} copy(f32[8,16,8,128]{3,2,1,0:T(8,128)} %update.1) | data formatting | bytes 1048576

commit v4 on v3

--- a/solution.py
+++ b/solution.py
@@ -64,14 +64,23 @@
     has_left = s > 0
     has_right = s < tiles - 1
     is_last = t == time_parts - 1
+    asks, says = (t == 0) & (s == mid - 1), is_last & (s == mid - 1)
 
     barrier = pltpu.get_barrier_semaphore()
 
     def greet(device):
         pl.semaphore_signal(barrier, inc=1, device_id=device, device_id_type=MESH)
 
-    greet((after, s))
     greet((sibling, s))
+
+    @pl.when(jnp.logical_not(says))
+    def _():
+        greet((after, s))
+
+    @pl.when(asks)
+    def _():
+        greet((before, s))
+
     for here, device in (
         (has_left, s - 1),
         (has_right, s + 1),
@@ -102,7 +111,7 @@
         )
 
     class Side:
-        def __init__(self, base, step, first, halo, inn, cel, cel_up, rat, relay, entry):
+        def __init__(self, base, step, first, halo, inn, cel, cel_up, rat, relay, entry, far):
             self.sends, self.receives = (has_right, has_left) if step > 0 else (has_left, has_right)
             self.zeros = (halo, inn, cel, cel_up, rat)
             to = (t, s + step)
@@ -133,18 +142,19 @@
                 remote(base + STATE + i, ac.at[i, :, cols], halo.at[i, :, cols], to)
                 for i in range(OWN, STEPS_DEV)
             ]
+            self.straight, self.far = [i for i in range(OWN) if i not in far], far
             self.detour = [
                 remote(base + STATE + i, a.at[i + DEPTH, :, cols], hold.at[i, :, cols], (t, relay), base + RELAY + i)
-                for i in range(OWN)
+                for i in far
             ]
             self.relayed = [
                 remote(base + RELAY + i, hold.at[i, :, cols], halo.at[i, :, cols], (t, entry + step), base + STATE + i)
-                for i in range(OWN)
+                for i in far
             ]
 
     sides = (
-        Side(0, 1, 3, hl, nl, kl, kl2, rl, tiles - 1, mid - 1),
-        Side(PER_SIDE, -1, 0, hr, nr, kr, kr2, rr, 0, mid),
+        Side(0, 1, 3, hl, nl, kl, kl2, rl, tiles - 1, mid - 1, (0, 1, 2)),
+        Side(PER_SIDE, -1, 0, hr, nr, kr, kr2, rr, 0, mid, (0, 1, 2)),
     )
     up_early = [
         remote(CELLS_T, cells, kc2, (before, s)),
@@ -180,33 +190,37 @@
     pl.semaphore_wait(
         barrier,
         2 + number(has_left) + number(has_right) + 2 * number(s == mid - 1) + number(s == mid)
-        + number(s == tiles - 1),
+        + number(s == tiles - 1) + number(says) - number(asks),
     )
 
     @pl.when(s == mid - 1)
     def _():
         pl.semaphore_signal(ready, inc=1, device_id=(t, 0), device_id_type=MESH)
 
-    for copy in up_early + up_state:
-        copy.start()
+    @pl.when(says)
+    def _():
+        pl.semaphore_signal(ready, inc=1, device_id=(after, s), device_id_type=MESH)
+
+    each(jnp.logical_not(asks), up_early + up_state, begin)
+    for side in sides:
+        for half in range(2):
+            each(side.sends & (core == half), side.rates[2 * half : 2 * half + 2], begin)
     for side in sides:
         each(side.sends, side.early, begin)
         each(side.is_entry, side.detour, begin)
-    for side in sides:
-        for half in range(2):
-            each(side.sends & (core == half), side.rates[2 * half : 2 * half + 2], begin)
 
     for load in loads:
         load.wait()
     for i in range(OWN):
         for side in sides:
-            each(side.sends & jnp.logical_not(side.is_entry), [side.state[i]], begin)
+            near = side.sends if i in side.straight else side.sends & jnp.logical_not(side.is_entry)
+            each(near, [side.state[i]], begin)
 
     def own_forcing(n, carry):
         fill_forcing(forcing, 0, n, [(nc[n], kc[pl.ds(n, 1)], 0, TX)])
         return carry
 
-    lax.fori_loop(0, STEPS_DEV, own_forcing, 0, unroll=4)
+    lax.fori_loop(0, STEPS_DEV, own_forcing, 0, unroll=8)
 
     def pass_on(first, last):
         if first == 0:
@@ -219,9 +233,28 @@
             for side in sides:
                 each(side.sends, [side.state[OWN + i]], begin)
 
+    def next_own_forcing(n, carry):
+        m = n + STEPS_DEV
+        fill_forcing(forcing, 0, m, [(nc[m], kc2[pl.ds(n, 1)], 0, TX)])
+        return carry
+
+    @pl.when(asks)
+    def _():
+        pl.semaphore_wait(ready, 1)
+        for copy in up_early + up_state:
+            copy.start()
+
     @pl.when(core == 0)
     def _():
         pass_on(0, DEPTH)
+        lax.fori_loop(0, 4, next_own_forcing, 0, unroll=4)
+
+    def relay(side):
+        for taken, given in zip(side.detour, side.relayed):
+            each(side.is_relay, [taken], arrive)
+            each(side.is_relay, [given], begin)
+
+    relay(sides[0])
 
     for side in sides:
         for half in range(2):
@@ -281,16 +314,10 @@
 
     lax.fori_loop(0, LEV, make_rates, 0, unroll=2)
 
-    def relay(side):
-        for i in range(OWN):
-            each(side.is_relay, [side.detour[i]], arrive)
-            each(side.is_relay, [side.relayed[i]], begin)
-
-    relay(sides[0])
-
     @pl.when(core == 1)
     def _():
         pass_on(0, 2)
+        lax.fori_loop(0, 4, next_own_forcing, 0, unroll=4)
 
     for side in sides:
         each(side.receives, side.early, arrive)
@@ -299,7 +326,7 @@
         fill_forcing(forcing, 1, n, [(nl[n], kl[pl.ds(n, 1)], 4, TX), (nr[n], kr[pl.ds(n, 1)], 0, 4)])
         return carry
 
-    lax.fori_loop(0, STEPS_DEV, halo_forcing, 0, unroll=4)
+    lax.fori_loop(0, STEPS_DEV, halo_forcing, 0, unroll=8)
 
     @pl.when(core == 1)
     def _():
@@ -312,10 +339,10 @@
     relay(sides[1])
 
 
-    def next_forcing(n):
+    def next_forcing(n, carry):
         m = n + STEPS_DEV
-        fill_forcing(forcing, 0, m, [(nc[m], kc2[pl.ds(n, 1)], 0, TX)])
         fill_forcing(forcing, 1, m, [(nl[m], kl2[pl.ds(n, 1)], 4, TX), (nr[m], kr2[pl.ds(n, 1)], 0, 4)])
+        return carry
 
     def sweep(first, loads, dst, plane, last):
         def level(l):
@@ -372,12 +399,7 @@
         def _():
             for side in sides:
                 each(side.receives, side.late, arrive)
-
-        for p in range(GROUP):
-
-            @pl.when(first + p > OWN)
-            def _(p=p):
-                next_forcing(first + p - OWN - 1)
+            lax.fori_loop(0, 4, next_forcing, 0, unroll=4)
 
         def start(p):
             return lambda l: (ac[first + p, l], (hl[first + p, l], hr[first + p, l]))
@@ -412,7 +434,8 @@
         pltpu.make_async_copy(ob.at[i], out.at[i], local.at[7 + i]).wait()
     for side in sides:
         each(side.sends, side.early + side.late + side.state[OWN:], leave)
-        each(side.sends & jnp.logical_not(side.is_entry), side.state[:OWN], leave)
+        each(side.sends, [side.state[i] for i in side.straight], leave)
+        each(side.sends & jnp.logical_not(side.is_entry), [side.state[i] for i in side.far], leave)
         each(side.is_entry, side.detour, leave)
         each(side.is_relay, side.relayed, leave)
         for half in range(2):

time: 28.7 us -> 26.1 us (0.909)
  the two profiles are of different devices: /device:TPU:2 before, /device:TPU:239 now
where the time goes in v4:
time: 26.1 us; the launch traced here: 25.9 us
  Pallas kernels  24 us (92%)
  local copies, waits for them, and re-layouts  1.87 us (7%)
    pallas_call x1, Pallas kernels, body(): pl.pallas_call(functools.partial(kernel, lax.axis_size('tm'), lax.axis_si...  24 us
    unnamed x1, local copies, waits for them, and re-layouts  1.87 us

profile of v4, /device:TPU:239, one launch (start us, length us, event | category | flops | bytes accessed | tf_op | source)
XLA Modules:
  0.0 25.9 jit_solution(7286972208345400760)
XLA Ops:
  0.0 24.0 %update.1 = f32[8,16,8,128]{3,2,1,0:T(8,128)} custom-call(f32[8,16,8,128]{3,2,1,0:T(8,128)} %a.1, f32[8,16,128]{2,1,0:T(8,128)} %innov.1, s32[8,128]{1,0:T(8,128)} %cells.1, f32[16,8,128]{2,1,0:T(8,128)} %dif.1, f32[16,8,128]{2,1,0:T(8,128)} %wx.1, f32[16,8,128]{2,1,0:T(8,128)} %wy.1, f32[16,8,128]{2,1,0:T(8,128)} %vm.1), custom_call_target="tpu_custom_call" | custom-call | tf_op jit(solution)/shard_map/update/pallas_call | solution.py:464
  24.0 1.9 %copy.9 = f32[8,16,8,128]{3,2,1,0:T(8,128)} copy(f32[8,16,8,128]{3,2,1,0:T(8,128)} %update.1) | data formatting | bytes 1048576

commit v5 on v4

--- a/solution.py
+++ b/solution.py
@@ -51,7 +51,7 @@
 def kernel(
     time_parts, tiles,
     a, innov, cells, dif, wx, wy, vm, out,
-    ac, hl, hr, nc, nl, nr, kc, kl, kr, kc2, kl2, kr2, rc, rl, rr, coef, forcing, va, vb, ob, hold,
+    ac, hl, hr, nc, nl, nr, kc, kl, kr, kc2, kl2, kr2, rc, rl, rr, coef, forcing, va, vb, hold,
     send, recv, local, ready,
 ):
     t = lax.axis_index("tm")
@@ -385,7 +385,7 @@
                         if 0 <= k < LEV:
                             total = total + levels[k][p][3][which]
                     if last:
-                        ob[first + p, l] = total
+                        out[first + p, l] = total
                     else:
                         dst[p, l, which] = total
 
@@ -424,14 +424,10 @@
                 return lambda l: (src[p, l, 0], src[p, l, 1])
 
             sweep(first, [middle(p) for p in range(GROUP)], dst, first + DEPTH - k, k == DEPTH)
-        for p in range(GROUP):
-            pltpu.make_async_copy(ob.at[first + p], out.at[first + p], local.at[7 + first + p]).start()
         return carry
 
     lax.fori_loop(0, STEPS_DEV // GROUP, chain, 0)
 
-    for i in range(STEPS_DEV):
-        pltpu.make_async_copy(ob.at[i], out.at[i], local.at[7 + i]).wait()
     for side in sides:
         each(side.sends, side.early + side.late + side.state[OWN:], leave)
         each(side.sends, [side.state[i] for i in side.straight], leave)
@@ -457,21 +453,24 @@
         + [pltpu.VMEM((LEV, 2, 6, TX, NY), f32)]
         + [pltpu.VMEM((STEPS_DEV + 4, LEV, 2, TX, NY), f32)]
         + [pltpu.VMEM((GROUP, LEV, 2, TX, NY), f32)] * 2
-        + [pltpu.VMEM((STEPS_DEV,) + field, f32), pltpu.VMEM((OWN,) + field, f32)]
+        + [pltpu.VMEM((OWN,) + field, f32)]
         + [pltpu.SemaphoreType.DMA((TRANSFERS,))] * 2
-        + [pltpu.SemaphoreType.DMA((7 + STEPS_DEV,)), pltpu.SemaphoreType.REGULAR]
+        + [pltpu.SemaphoreType.DMA((7,)), pltpu.SemaphoreType.REGULAR]
     )
     return pl.pallas_call(
         functools.partial(kernel, lax.axis_size("tm"), lax.axis_size("space")),
         out_shape=jax.ShapeDtypeStruct((STEPS_DEV,) + field, f32),
         in_specs=[pl.BlockSpec(memory_space=pl.ANY)] * 7,
-        out_specs=pl.BlockSpec(memory_space=pl.ANY),
+        out_specs=pl.BlockSpec(memory_space=pltpu.VMEM),
         scratch_shapes=scratch,
         compiler_params=pltpu.CompilerParams(
-            collective_id=0, has_side_effects=True, vmem_limit_bytes=62 * 2**20
+            collective_id=0, has_side_effects=True, vmem_limit_bytes=24 * 2**20
         ),
         name="update",
-    )(adjoint_iterate, innovations, station_cells, diffusivity, wind_x, wind_y, vertical_mixing)
+    )(*[
+        pltpu.with_memory_space_constraint(x, pltpu.HBM)
+        for x in (adjoint_iterate, innovations, station_cells, diffusivity, wind_x, wind_y, vertical_mixing)
+    ])
 
 
 def solution(mesh):

time: 26.1 us -> 24.2 us (0.927)
  local copies, waits for them, and re-layouts: 1.87 us -> 0.8 us
  Pallas kernels: 24 us -> 23.3 us
    unnamed x1, local copies, waits for them, and re-layouts: 1.87 us -> 0.8 us
    pallas_call x1, Pallas kernels: 24 us -> 23.3 us  [body(): pl.pallas_call(functools.partial(kernel, lax.axis_size('tm'), lax.axis_si...]
where the time goes in v5:
time: 24.2 us; the launch traced here: 24.1 us
  Pallas kernels  23.3 us (96%)
  local copies, waits for them, and re-layouts  0.8 us (3%)
    pallas_call x1, Pallas kernels, body(): pl.pallas_call(functools.partial(kernel, lax.axis_size('tm'), lax.axis_si...  23.3 us
    unnamed x1, local copies, waits for them, and re-layouts  0.8 us

profile of v5, /device:TPU:239, one launch (start us, length us, event | category | flops | bytes accessed | tf_op | source)
XLA Modules:
  0.0 24.1 jit_solution(4226038302005553265)
XLA Ops:
  0.0 23.3 %update.1 = f32[8,16,8,128]{3,2,1,0:T(8,128)S(1)} custom-call(f32[8,16,8,128]{3,2,1,0:T(8,128)} %a.1, f32[8,16,128]{2,1,0:T(8,128)} %innov.1, s32[8,128]{1,0:T(8,128)} %cells.1, f32[16,8,128]{2,1,0:T(8,128)} %dif.1, f32[16,8,128]{2,1,0:T(8,128)} %wx.1, f32[16,8,128]{2,1,0:T(8,128)} %wy.1, f32[16,8,128]{2,1,0:T(8,128)} %vm.1), custom_call_target="tpu_custom_call" | custom-call | tf_op jit(solution)/shard_map/update/pallas_call | solution.py:460
  23.3 0.8 %copy.9 = f32[8,16,8,128]{3,2,1,0:T(8,128)} copy(f32[8,16,8,128]{3,2,1,0:T(8,128)S(1)} %update.1) | data formatting | bytes 1048576

commit v6 on v5

--- a/solution.py
+++ b/solution.py
@@ -64,7 +64,7 @@
     has_left = s > 0
     has_right = s < tiles - 1
     is_last = t == time_parts - 1
-    asks, says = (t == 0) & (s == mid - 1), is_last & (s == mid - 1)
+    asks, says = (core == 0) & (s == mid - 1), (core == 1) & (s == mid - 1)
 
     barrier = pltpu.get_barrier_semaphore()
 
@@ -206,7 +206,7 @@
         for half in range(2):
             each(side.sends & (core == half), side.rates[2 * half : 2 * half + 2], begin)
     for side in sides:
-        each(side.sends, side.early, begin)
+        each(side.sends if side is sides[0] else side.sends & (s != mid), side.early, begin)
         each(side.is_entry, side.detour, begin)
 
     for load in loads:
@@ -221,17 +221,22 @@
         return carry
 
     lax.fori_loop(0, STEPS_DEV, own_forcing, 0, unroll=8)
+    each(s == mid, sides[1].early, begin)
+
+    yields = s == mid
+
+    sides[0].goes, sides[1].goes = has_right, has_left & jnp.logical_not(yields)
 
     def pass_on(first, last):
         if first == 0:
             for copy in up_early:
                 copy.wait_recv()
             for side in sides:
-                each(side.sends, side.late, begin)
+                each(side.goes, side.late, begin)
         for i in range(first, last):
             up_state[i].wait_recv()
             for side in sides:
-                each(side.sends, [side.state[OWN + i]], begin)
+                each(side.goes, [side.state[OWN + i]], begin)
 
     def next_own_forcing(n, carry):
         m = n + STEPS_DEV
@@ -331,6 +336,8 @@
     @pl.when(core == 1)
     def _():
         pass_on(2, DEPTH)
+
+    each(yields, sides[1].late + sides[1].state[OWN:], begin)
 
     @pl.when(s == 0)
     def _():

time: 24.2 us -> 23.5 us (0.971)
  the two profiles are of different devices: /device:TPU:239 before, /device:TPU:3 now
where the time goes in v6:
time: 23.5 us
  Pallas kernels  22.6 us (96%)
  local copies, waits for them, and re-layouts  0.8 us (3%)
    pallas_call x1, Pallas kernels, body(): pl.pallas_call(functools.partial(kernel, lax.axis_size('tm'), lax.axis_si...  22.6 us
    unnamed x1, local copies, waits for them, and re-layouts  0.8 us

profile of v6, /device:TPU:3, one launch (start us, length us, event | category | flops | bytes accessed | tf_op | source)
XLA Modules:
  0.0 23.5 jit_solution(670258560816778058)
XLA Ops:
  0.0 22.6 %update.1 = f32[8,16,8,128]{3,2,1,0:T(8,128)S(1)} custom-call(f32[8,16,8,128]{3,2,1,0:T(8,128)} %a.1, f32[8,16,128]{2,1,0:T(8,128)} %innov.1, s32[8,128]{1,0:T(8,128)} %cells.1, f32[16,8,128]{2,1,0:T(8,128)} %dif.1, f32[16,8,128]{2,1,0:T(8,128)} %wx.1, f32[16,8,128]{2,1,0:T(8,128)} %wy.1, f32[16,8,128]{2,1,0:T(8,128)} %vm.1), custom_call_target="tpu_custom_call" | custom-call | tf_op jit(solution)/shard_map/update/pallas_call | solution.py:467
  22.7 0.8 %copy.9 = f32[8,16,8,128]{3,2,1,0:T(8,128)} copy(f32[8,16,8,128]{3,2,1,0:T(8,128)S(1)} %update.1) | data formatting | bytes 1048576

commit v7 on v6

--- a/solution.py
+++ b/solution.py
@@ -321,7 +321,7 @@
 
     @pl.when(core == 1)
     def _():
-        pass_on(0, 2)
+        pass_on(0, 4)
         lax.fori_loop(0, 4, next_own_forcing, 0, unroll=4)
 
     for side in sides:
@@ -335,7 +335,7 @@
 
     @pl.when(core == 1)
     def _():
-        pass_on(2, DEPTH)
+        pass_on(4, DEPTH)
 
     each(yields, sides[1].late + sides[1].state[OWN:], begin)
 
@@ -398,15 +398,16 @@
 
     def chain(group, carry):
         first = group * GROUP
-        for k in range(STEPS_DEV):
-            for side in sides:
-                each(side.receives & (group == k // GROUP), [side.state[k]], arrive)
-
-        @pl.when(group == (OWN + 1) // GROUP)
+
+        @pl.when(group == OWN // GROUP)
         def _():
             for side in sides:
                 each(side.receives, side.late, arrive)
             lax.fori_loop(0, 4, next_forcing, 0, unroll=4)
+
+        for k in range(STEPS_DEV):
+            for side in sides:
+                each(side.receives & (group == k // GROUP), [side.state[k]], arrive)
 
         def start(p):
             return lambda l: (ac[first + p, l], (hl[first + p, l], hr[first + p, l]))

time: 23.5 us -> 23.2 us (0.987)
  Pallas kernels: 22.6 us -> 22.3 us
    pallas_call x1, Pallas kernels: 22.6 us -> 22.3 us  [body(): pl.pallas_call(functools.partial(kernel, lax.axis_size('tm'), lax.axis_si...]
where the time goes in v7:
time: 23.2 us; the launch traced here: 23.1 us
  Pallas kernels  22.3 us (96%)
  local copies, waits for them, and re-layouts  0.8 us (3%)
    pallas_call x1, Pallas kernels, body(): pl.pallas_call(functools.partial(kernel, lax.axis_size('tm'), lax.axis_si...  22.3 us
    unnamed x1, local copies, waits for them, and re-layouts  0.8 us

profile of v7, /device:TPU:3, one launch (start us, length us, event | category | flops | bytes accessed | tf_op | source)
XLA Modules:
  0.0 23.1 jit_solution(12558200613958457373)
XLA Ops:
  0.0 22.3 %update.1 = f32[8,16,8,128]{3,2,1,0:T(8,128)S(1)} custom-call(f32[8,16,8,128]{3,2,1,0:T(8,128)} %a.1, f32[8,16,128]{2,1,0:T(8,128)} %innov.1, s32[8,128]{1,0:T(8,128)} %cells.1, f32[16,8,128]{2,1,0:T(8,128)} %dif.1, f32[16,8,128]{2,1,0:T(8,128)} %wx.1, f32[16,8,128]{2,1,0:T(8,128)} %wy.1, f32[16,8,128]{2,1,0:T(8,128)} %vm.1), custom_call_target="tpu_custom_call" | custom-call | tf_op jit(solution)/shard_map/update/pallas_call | solution.py:468
  22.3 0.8 %copy.9 = f32[8,16,8,128]{3,2,1,0:T(8,128)} copy(f32[8,16,8,128]{3,2,1,0:T(8,128)S(1)} %update.1) | data formatting | bytes 1048576

commit v8 on v7

--- a/solution.py
+++ b/solution.py
@@ -243,16 +243,16 @@
         fill_forcing(forcing, 0, m, [(nc[m], kc2[pl.ds(n, 1)], 0, TX)])
         return carry
 
+    @pl.when(core == 0)
+    def _():
+        pass_on(0, DEPTH)
+        lax.fori_loop(0, 4, next_own_forcing, 0, unroll=4)
+
     @pl.when(asks)
     def _():
         pl.semaphore_wait(ready, 1)
         for copy in up_early + up_state:
             copy.start()
-
-    @pl.when(core == 0)
-    def _():
-        pass_on(0, DEPTH)
-        lax.fori_loop(0, 4, next_own_forcing, 0, unroll=4)
 
     def relay(side):
         for taken, given in zip(side.detour, side.relayed):

time: 23.2 us -> 23.2 us (level)
  no operation moved by 1% of the time
where the time goes in v8:
time: 23.2 us; the launch traced here: 23.1 us
  Pallas kernels  22.3 us (96%)
  local copies, waits for them, and re-layouts  0.8 us (3%)
    pallas_call x1, Pallas kernels, body(): pl.pallas_call(functools.partial(kernel, lax.axis_size('tm'), lax.axis_si...  22.3 us
    unnamed x1, local copies, waits for them, and re-layouts  0.8 us

profile of v8, /device:TPU:3, one launch (start us, length us, event | category | flops | bytes accessed | tf_op | source)
XLA Modules:
  0.0 23.1 jit_solution(13983605769549894167)
XLA Ops:
  0.0 22.3 %update.1 = f32[8,16,8,128]{3,2,1,0:T(8,128)S(1)} custom-call(f32[8,16,8,128]{3,2,1,0:T(8,128)} %a.1, f32[8,16,128]{2,1,0:T(8,128)} %innov.1, s32[8,128]{1,0:T(8,128)} %cells.1, f32[16,8,128]{2,1,0:T(8,128)} %dif.1, f32[16,8,128]{2,1,0:T(8,128)} %wx.1, f32[16,8,128]{2,1,0:T(8,128)} %wy.1, f32[16,8,128]{2,1,0:T(8,128)} %vm.1), custom_call_target="tpu_custom_call" | custom-call | tf_op jit(solution)/shard_map/update/pallas_call | solution.py:468
  22.3 0.8 %copy.9 = f32[8,16,8,128]{3,2,1,0:T(8,128)} copy(f32[8,16,8,128]{3,2,1,0:T(8,128)S(1)} %update.1) | data formatting | bytes 1048576
